TPU v7x, 32 devices: a whole 2x2x4 slice. The times are simulated.
32 devices in a mesh: rep: 4 (over x, core), ctx: 8 (over z, y).
Axes of the slice: x: 2, y: 2, z: 4, core: 2. Of those that a mesh axis runs over, the one named last changes fastest.
Arguments:
- tokens: bfloat16 [8, 1024, 1536], P('rep', 'ctx'), may hold values from -6 to 6
- cotangent: bfloat16 [8, 1024, 1536], P('rep', 'ctx'), may hold values from -6 to 6
- query_weight: float32 [1536, 1536], P('ctx'), may hold values from -0.15625 to 0.15625
- key_weight: float32 [1536, 512], P('ctx'), may hold values from -0.15625 to 0.15625
- value_weight: float32 [1536, 512], P('ctx'), may hold values from -0.15625 to 0.15625
- output_weight: float32 [1536, 1536], P('ctx'), may hold values from -0.625 to 0.625
- gate_weight: float32 [1536, 6912], P('ctx'), may hold values from -0.15625 to 0.15625
- up_weight: float32 [1536, 6912], P('ctx'), may hold values from -0.15625 to 0.15625
- down_weight: float32 [6912, 1536], P('ctx'), may hold values from -0.078125 to 0.078125
- norm_gains: float32 [1600, 2], P('ctx'), may hold values from 0.5 to 1.5
- first_query: float32 [1536, 1536], P('ctx'), may hold values from -24 to 24
- first_key: float32 [1536, 512], P('ctx'), may hold values from -32 to 32
- first_value: float32 [1536, 512], P('ctx'), may hold values from -32 to 32
- first_output: float32 [1536, 1536], P('ctx'), may hold values from -6 to 6
- first_gate: float32 [1536, 6912], P('ctx'), may hold values from -32 to 32
- first_up: float32 [1536, 6912], P('ctx'), may hold values from -32 to 32
- first_down: float32 [6912, 1536], P('ctx'), may hold values from -32 to 32
- first_gains: float32 [1600, 2], P('ctx'), may hold values from -80 to 80
- second_query: float32 [1536, 1536], P('ctx'), may hold values from 69.632 to 278.528
- second_key: float32 [1536, 512], P('ctx'), may hold values from 106.496 to 425.984
- second_value: float32 [1536, 512], P('ctx'), may hold values from 155.648 to 622.592
- second_output: float32 [1536, 1536], P('ctx'), may hold values from 3.84 to 15.2
- second_gate: float32 [1536, 6912], P('ctx'), may hold values from 155.648 to 622.592
- second_up: float32 [1536, 6912], P('ctx'), may hold values from 155.648 to 622.592
- second_down: float32 [6912, 1536], P('ctx'), may hold values from 155.648 to 622.592
- second_gains: float32 [1600, 2], P('ctx'), may hold values from 737.28 to 2949.12
Outputs:
- activations: bfloat16 [8, 1024, 1536], P('rep', 'ctx')
- input_gradient: float32 [8, 1024, 1536], P('rep', 'ctx')
- query_new: float32 [1536, 1536], P('ctx')
- key_new: float32 [1536, 512], P('ctx')
- value_new: float32 [1536, 512], P('ctx')
- output_new: float32 [1536, 1536], P('ctx')
- gate_new: float32 [1536, 6912], P('ctx')
- up_new: float32 [1536, 6912], P('ctx')
- down_new: float32 [6912, 1536], P('ctx')
- gains_new: float32 [1600, 2], P('ctx')
- first_query_new: float32 [1536, 1536], P('ctx')
- first_key_new: float32 [1536, 512], P('ctx')
- first_value_new: float32 [1536, 512], P('ctx')
- first_output_new: float32 [1536, 1536], P('ctx')
- first_gate_new: float32 [1536, 6912], P('ctx')
- first_up_new: float32 [1536, 6912], P('ctx')
- first_down_new: float32 [6912, 1536], P('ctx')
- first_gains_new: float32 [1600, 2], P('ctx')
- second_query_new: float32 [1536, 1536], P('ctx')
- second_key_new: float32 [1536, 512], P('ctx')
- second_value_new: float32 [1536, 512], P('ctx')
- second_output_new: float32 [1536, 1536], P('ctx')
- second_gate_new: float32 [1536, 6912], P('ctx')
- second_up_new: float32 [1536, 6912], P('ctx')
- second_down_new: float32 [6912, 1536], P('ctx')
- second_gains_new: float32 [1600, 2], P('ctx')
All inputs are finite; a program needn't handle non-finite values.
Results may differ from a plain program's by a relative error of at most 0.025.
Values may be sent and summed in bfloat16 or wider, within the bound.
A program may use at most 448 MiB of HBM per device.

v0:
```python
import jax
import jax.numpy as jnp
from jax import lax
from jax.sharding import PartitionSpec as P

HD = 64
STEP = 5


norm_eps = 1e-05
rope_base = 1000000.0
score_scale = 0.125
beta_one = 0.9
beta_two = 0.95
adam_eps = 1e-08


def product(left, right):
    return jnp.dot(left, right, preferred_element_type=jnp.float32)


def product_back(left, right):
    return lax.dot_general(
        left, right, (((1,), (1,)), ((), ())), preferred_element_type=jnp.float32
    )


def product_rows(left, right):
    return lax.dot_general(
        left, right, (((0,), (0,)), ((), ())), preferred_element_type=jnp.float32
    )


def rms_scale(values):
    return lax.rsqrt(jnp.mean(values * values, axis=-1, keepdims=True) + norm_eps)


def norm_back(grad, values, gain):
    scale = rms_scale(values)
    scaled = grad * gain
    inner = jnp.mean(scaled * values, axis=-1, keepdims=True)
    return (scale * scaled - values * (scale * scale * scale) * inner, grad * values * scale)


def rotary_tables(start, count, head_dim):
    half = head_dim // 2
    inverse = jnp.power(
        jnp.float32(rope_base), -(jnp.arange(half).astype(jnp.float32) * 2.0) / head_dim
    )
    angle = (start + jnp.arange(count)).astype(jnp.float32)[:, None] * inverse[None, :]
    return (jnp.cos(angle), jnp.sin(angle))


def rotate(values, cosine, sine):
    half = values.shape[-1] // 2
    first = values[..., :half]
    second = values[..., half:]
    cosine = cosine[:, None, :]
    sine = sine[:, None, :]
    return jnp.concatenate(
        [first * cosine - second * sine, second * cosine + first * sine], axis=-1
    )


def rotate_back(grads, cosine, sine):
    half = grads.shape[-1] // 2
    first = grads[..., :half]
    second = grads[..., half:]
    cosine = cosine[:, None, :]
    sine = sine[:, None, :]
    return jnp.concatenate(
        [first * cosine + second * sine, second * cosine - first * sine], axis=-1
    )


def adamw(weight, grad, first, second, rate, decay):
    first_new = beta_one * first + (1.0 - beta_one) * grad
    second_new = beta_two * second + (1.0 - beta_two) * grad * grad
    fix_one = 1.0 - beta_one**STEP
    fix_two = 1.0 - beta_two**STEP
    update = first_new / fix_one / (jnp.sqrt(second_new / fix_two) + adam_eps)
    return (weight - rate * (update + decay * weight), first_new, second_new)


def body(
    tokens,
    cotangent,
    query_weight,
    key_weight,
    value_weight,
    output_weight,
    gate_weight,
    up_weight,
    down_weight,
    norm_gains,
    first_query,
    first_key,
    first_value,
    first_output,
    first_gate,
    first_up,
    first_down,
    first_gains,
    second_query,
    second_key,
    second_value,
    second_output,
    second_gate,
    second_up,
    second_down,
    second_gains,
):
    seqs, span, width = tokens.shape
    rows = seqs * span
    head_dim = HD
    heads = query_weight.shape[1] // head_dim
    kv_heads = key_weight.shape[1] // head_dim
    group = heads // kv_heads
    kv_width = kv_heads * head_dim
    parts = lax.axis_size("ctx")
    place = lax.axis_index("ctx")
    length = span * parts
    query_shard = query_weight.astype(jnp.bfloat16)
    key_shard = key_weight.astype(jnp.bfloat16)
    value_shard = value_weight.astype(jnp.bfloat16)
    output_shard = output_weight.astype(jnp.bfloat16)
    gains_shard = norm_gains.astype(jnp.bfloat16)
    gate_shard = gate_weight.astype(jnp.bfloat16)
    up_shard = up_weight.astype(jnp.bfloat16)
    down_shard = down_weight.astype(jnp.bfloat16)
    w_query, w_key, w_value, w_output, gains_low = (
        lax.all_gather(query_shard, "ctx", axis=0, tiled=True),
        lax.all_gather(key_shard, "ctx", axis=0, tiled=True),
        lax.all_gather(value_shard, "ctx", axis=0, tiled=True),
        lax.all_gather(output_shard, "ctx", axis=0, tiled=True),
        lax.all_gather(gains_shard, "ctx", axis=0, tiled=True),
    )
    w_gate, w_up, w_down = (
        lax.all_gather(gate_shard, "ctx", axis=0, tiled=True),
        lax.all_gather(up_shard, "ctx", axis=0, tiled=True),
        lax.all_gather(down_shard, "ctx", axis=0, tiled=True),
    )
    gains_full = gains_low.astype(jnp.float32)
    gain_attn = gains_full[:width, 0]
    gain_ffn = gains_full[:width, 1]
    gain_query = gains_full[width:, 0]
    gain_key = gains_full[width:, 1]
    inputs = tokens.astype(jnp.float32).reshape(rows, width)
    normed_one = (inputs * rms_scale(inputs) * gain_attn).astype(jnp.bfloat16)
    query_lin = product(normed_one, w_query)
    key_lin = product(normed_one, w_key)
    value_low = product(normed_one, w_value).astype(jnp.bfloat16)
    cosine, sine = rotary_tables(place * span, span, head_dim)
    query_heads = query_lin.reshape(seqs, span, heads, head_dim)
    query_low = rotate(query_heads * rms_scale(query_heads) * gain_query, cosine, sine).astype(
        jnp.bfloat16
    )
    key_heads = key_lin.reshape(seqs, span, kv_heads, head_dim)
    key_low = rotate(key_heads * rms_scale(key_heads) * gain_key, cosine, sine).astype(jnp.bfloat16)
    keys_all, values_all = (
        lax.all_gather(key_low.reshape(seqs, span, kv_width), "ctx", axis=1, tiled=True),
        lax.all_gather(value_low.reshape(seqs, span, kv_width), "ctx", axis=1, tiled=True),
    )
    query_grouped = query_low.reshape(seqs, span, kv_heads, group, head_dim)
    query_pos = place * span + jnp.arange(span)
    visible = jnp.arange(length)[None, :] <= query_pos[:, None]

    def head_scores(index):
        query_group = lax.dynamic_index_in_dim(query_grouped, index, 2, keepdims=False)
        key_group = lax.dynamic_slice_in_dim(keys_all, index * head_dim, head_dim, 2)
        value_group = lax.dynamic_slice_in_dim(values_all, index * head_dim, head_dim, 2)
        raw = (
            jnp.einsum("scjd,skd->sjck", query_group, key_group, preferred_element_type=jnp.float32)
            * score_scale
        )
        return (query_group, key_group, value_group, jnp.where(visible, raw, -1e30))

    def forward_head(index, carry):
        attended, log_sums = carry
        query_group, key_group, value_group, scores = head_scores(index)
        top = jnp.max(scores, axis=-1, keepdims=True)
        expo = jnp.exp(scores - top)
        total = jnp.sum(expo, axis=-1, keepdims=True)
        probs = (expo / total).astype(jnp.bfloat16)
        head_out = jnp.einsum(
            "sjck,skd->scjd", probs, value_group, preferred_element_type=jnp.float32
        )
        attended = lax.dynamic_update_index_in_dim(attended, head_out, index, 2)
        log_sums = lax.dynamic_update_index_in_dim(
            log_sums, (top + jnp.log(total))[..., 0], index, 0
        )
        return (attended, log_sums)

    attended, log_sums = lax.fori_loop(
        0,
        kv_heads,
        forward_head,
        (
            jnp.zeros((seqs, span, kv_heads, group, head_dim), jnp.float32),
            jnp.zeros((kv_heads, seqs, group, span), jnp.float32),
        ),
    )
    attended_low = attended.reshape(rows, heads * head_dim).astype(jnp.bfloat16)
    resid = inputs + product(attended_low, w_output)
    normed_two = (resid * rms_scale(resid) * gain_ffn).astype(jnp.bfloat16)
    gate = product(normed_two, w_gate)
    up = product(normed_two, w_up)
    sigma = jax.nn.sigmoid(gate)
    hidden_low = (gate * sigma * up).astype(jnp.bfloat16)
    activations = (
        (resid + product(hidden_low, w_down)).astype(jnp.bfloat16).reshape(seqs, span, width)
    )
    w_gate, w_up, w_down = (
        lax.all_gather(gate_shard, "ctx", axis=0, tiled=True),
        lax.all_gather(up_shard, "ctx", axis=0, tiled=True),
        lax.all_gather(down_shard, "ctx", axis=0, tiled=True),
    )
    grad_out = cotangent.astype(jnp.float32).reshape(rows, width)
    grad_low = grad_out.astype(jnp.bfloat16)
    grad_hidden = product_back(grad_low, w_down)
    up_grad_low = (grad_hidden * gate * sigma).astype(jnp.bfloat16)
    gate_grad_low = (grad_hidden * up * sigma * (1.0 + gate * (1.0 - sigma))).astype(jnp.bfloat16)
    down_grad = lax.psum_scatter(
        product_rows(hidden_low, grad_low).astype(jnp.bfloat16),
        "ctx",
        scatter_dimension=0,
        tiled=True,
    )
    gate_grad = lax.psum_scatter(
        product_rows(normed_two, gate_grad_low).astype(jnp.bfloat16),
        "ctx",
        scatter_dimension=0,
        tiled=True,
    )
    up_grad = lax.psum_scatter(
        product_rows(normed_two, up_grad_low).astype(jnp.bfloat16),
        "ctx",
        scatter_dimension=0,
        tiled=True,
    )
    normed_two_grad = product_back(gate_grad_low, w_gate) + product_back(up_grad_low, w_up)
    back_two, ffn_terms = norm_back(normed_two_grad, resid, gain_ffn)
    grad_resid = grad_out + back_two
    resid_low = grad_resid.astype(jnp.bfloat16)
    output_term = product_rows(attended_low, resid_low)
    w_query, w_key, w_value, w_output, gains_low = (
        lax.all_gather(query_shard, "ctx", axis=0, tiled=True),
        lax.all_gather(key_shard, "ctx", axis=0, tiled=True),
        lax.all_gather(value_shard, "ctx", axis=0, tiled=True),
        lax.all_gather(output_shard, "ctx", axis=0, tiled=True),
        lax.all_gather(gains_shard, "ctx", axis=0, tiled=True),
    )
    grad_grouped = (
        product_back(resid_low, w_output)
        .astype(jnp.bfloat16)
        .reshape(seqs, span, kv_heads, group, head_dim)
    )

    def backward_head(index, carry):
        query_acc, key_acc, value_acc = carry
        query_group, key_group, value_group, scores = head_scores(index)
        log_group = lax.dynamic_index_in_dim(log_sums, index, 0, keepdims=False)
        probs = jnp.exp(scores - log_group[..., None])
        grad_group = lax.dynamic_index_in_dim(grad_grouped, index, 2, keepdims=False)
        grad_probs = jnp.einsum(
            "scjd,skd->sjck", grad_group, value_group, preferred_element_type=jnp.float32
        )
        inner = jnp.sum(probs * grad_probs, axis=-1, keepdims=True)
        grad_scores = (probs * (grad_probs - inner)).astype(jnp.bfloat16)
        grad_query = (
            jnp.einsum("sjck,skd->scjd", grad_scores, key_group, preferred_element_type=jnp.float32)
            * score_scale
        )
        grad_key = (
            jnp.einsum(
                "sjck,scjd->skd", grad_scores, query_group, preferred_element_type=jnp.float32
            )
            * score_scale
        )
        grad_value = jnp.einsum(
            "sjck,scjd->skd",
            probs.astype(jnp.bfloat16),
            grad_group,
            preferred_element_type=jnp.float32,
        )
        query_acc = lax.dynamic_update_index_in_dim(query_acc, grad_query, index, 2)
        key_acc = lax.dynamic_update_slice_in_dim(key_acc, grad_key, index * head_dim, 2)
        value_acc = lax.dynamic_update_slice_in_dim(value_acc, grad_value, index * head_dim, 2)
        return (query_acc, key_acc, value_acc)

    query_acc, key_acc, value_acc = lax.fori_loop(
        0,
        kv_heads,
        backward_head,
        (
            jnp.zeros((seqs, span, kv_heads, group, head_dim), jnp.float32),
            jnp.zeros((seqs, length, kv_width), jnp.float32),
            jnp.zeros((seqs, length, kv_width), jnp.float32),
        ),
    )
    key_back, value_back = (
        lax.psum_scatter(
            key_acc.astype(jnp.bfloat16), "ctx", scatter_dimension=1, tiled=True
        ).astype(jnp.float32),
        lax.psum_scatter(
            value_acc.astype(jnp.bfloat16), "ctx", scatter_dimension=1, tiled=True
        ).astype(jnp.float32),
    )
    query_rot = rotate_back(query_acc.reshape(seqs, span, heads, head_dim), cosine, sine)
    query_back, query_gain_terms = norm_back(query_rot, query_heads, gain_query)
    key_rot = rotate_back(key_back.reshape(seqs, span, kv_heads, head_dim), cosine, sine)
    key_grad_back, key_gain_terms = norm_back(key_rot, key_heads, gain_key)
    query_grad_low = query_back.reshape(rows, heads * head_dim).astype(jnp.bfloat16)
    key_grad_low = key_grad_back.reshape(rows, kv_width).astype(jnp.bfloat16)
    value_grad_low = value_back.reshape(rows, kv_width).astype(jnp.bfloat16)
    query_term = product_rows(normed_one, query_grad_low)
    key_term = product_rows(normed_one, key_grad_low)
    value_term = product_rows(normed_one, value_grad_low)
    normed_one_grad = (
        product_back(query_grad_low, w_query)
        + product_back(key_grad_low, w_key)
        + product_back(value_grad_low, w_value)
    )
    back_one, attn_terms = norm_back(normed_one_grad, inputs, gain_attn)
    input_gradient = (grad_resid + back_one).reshape(seqs, span, width)
    column_one = jnp.concatenate(
        [jnp.sum(attn_terms, axis=0), jnp.sum(query_gain_terms, axis=(0, 1, 2))]
    )
    column_two = jnp.concatenate(
        [jnp.sum(ffn_terms, axis=0), jnp.sum(key_gain_terms, axis=(0, 1, 2))]
    )
    gains_term = jnp.stack([column_one, column_two], axis=1)
    query_part, key_part, value_part, output_part, gains_part = (
        lax.psum_scatter(
            query_term.astype(jnp.bfloat16), "ctx", scatter_dimension=0, tiled=True
        ).astype(jnp.float32),
        lax.psum_scatter(
            key_term.astype(jnp.bfloat16), "ctx", scatter_dimension=0, tiled=True
        ).astype(jnp.float32),
        lax.psum_scatter(
            value_term.astype(jnp.bfloat16), "ctx", scatter_dimension=0, tiled=True
        ).astype(jnp.float32),
        lax.psum_scatter(
            output_term.astype(jnp.bfloat16), "ctx", scatter_dimension=0, tiled=True
        ).astype(jnp.float32),
        lax.psum_scatter(
            gains_term.astype(jnp.bfloat16), "ctx", scatter_dimension=0, tiled=True
        ).astype(jnp.float32),
    )
    grads = (
        lax.psum(query_part.astype(jnp.bfloat16), "rep").astype(jnp.float32),
        lax.psum(key_part.astype(jnp.bfloat16), "rep").astype(jnp.float32),
        lax.psum(value_part.astype(jnp.bfloat16), "rep").astype(jnp.float32),
        lax.psum(output_part.astype(jnp.bfloat16), "rep").astype(jnp.float32),
        lax.psum(gate_grad, "rep").astype(jnp.float32),
        lax.psum(up_grad, "rep").astype(jnp.float32),
        lax.psum(down_grad, "rep").astype(jnp.float32),
        lax.psum(gains_part.astype(jnp.bfloat16), "rep").astype(jnp.float32),
    )
    weights = (
        query_weight,
        key_weight,
        value_weight,
        output_weight,
        gate_weight,
        up_weight,
        down_weight,
        norm_gains,
    )
    firsts = (
        first_query,
        first_key,
        first_value,
        first_output,
        first_gate,
        first_up,
        first_down,
        first_gains,
    )
    seconds = (
        second_query,
        second_key,
        second_value,
        second_output,
        second_gate,
        second_up,
        second_down,
        second_gains,
    )
    rates = (0.05, 0.05, 0.05, 0.3, 0.05, 0.05, 0.05, 0.5)
    decays = (0.1, 0.1, 0.1, 0.1, 0.1, 0.1, 0.1, 0.0)
    updated = [
        adamw(w, g, m, u, rate, decay)
        for w, g, m, u, rate, decay in zip(weights, grads, firsts, seconds, rates, decays)
    ]
    return (
        activations,
        input_gradient,
        updated[0][0],
        updated[1][0],
        updated[2][0],
        updated[3][0],
        updated[4][0],
        updated[5][0],
        updated[6][0],
        updated[7][0],
        updated[0][1],
        updated[1][1],
        updated[2][1],
        updated[3][1],
        updated[4][1],
        updated[5][1],
        updated[6][1],
        updated[7][1],
        updated[0][2],
        updated[1][2],
        updated[2][2],
        updated[3][2],
        updated[4][2],
        updated[5][2],
        updated[6][2],
        updated[7][2],
    )


def solution(mesh):
    placed = (
        P("rep", "ctx", None),
        P("rep", "ctx", None),
        P("ctx", None),
        P("ctx", None),
        P("ctx", None),
        P("ctx", None),
        P("ctx", None),
        P("ctx", None),
        P("ctx", None),
        P("ctx", None),
        P("ctx", None),
        P("ctx", None),
        P("ctx", None),
        P("ctx", None),
        P("ctx", None),
        P("ctx", None),
        P("ctx", None),
        P("ctx", None),
        P("ctx", None),
        P("ctx", None),
        P("ctx", None),
        P("ctx", None),
        P("ctx", None),
        P("ctx", None),
        P("ctx", None),
        P("ctx", None),
    )
    return jax.shard_map(
        body,
        mesh=mesh,
        in_specs=placed,
        out_specs=(
            P("rep", "ctx", None),
            P("rep", "ctx", None),
            P("ctx", None),
            P("ctx", None),
            P("ctx", None),
            P("ctx", None),
            P("ctx", None),
            P("ctx", None),
            P("ctx", None),
            P("ctx", None),
            P("ctx", None),
            P("ctx", None),
            P("ctx", None),
            P("ctx", None),
            P("ctx", None),
            P("ctx", None),
            P("ctx", None),
            P("ctx", None),
            P("ctx", None),
            P("ctx", None),
            P("ctx", None),
            P("ctx", None),
            P("ctx", None),
            P("ctx", None),
            P("ctx", None),
            P("ctx", None),
        ),
        check_vma=False,
    )
```

profile of v0, /device:TPU:0, one launch (start us, length us, event | category | flops | bytes accessed | tf_op | source)
XLA Modules:
  0.0 3497.5 jit_solution(7388516409420666127)
XLA Ops:
  11.9 22.4 all-gather
  36.9 20.6 all-gather.15.cloned.1.call-done
  62.0 41.3 %all-gather.11.cloned.1.call-done = bf16[1536,512]{1,0:T(8,128)(2,1)} async-done(((bf16[192,512]{1,0:T(8,128)(2,1)}), bf16[1536,512]{1,0:T(8,128)(2,1)}) %all-gather.11.cloned.1.call-update) | async-done | bytes 1572880 | tf_op jit(solution)/shard_map/all_gather | solution.py:134
  108.8 4.3 convert_element_type.215
  113.2 4.5 convert_element_type.216
  117.7 4.3 convert_element_type.218
  122.4 62.4 %all-gather.19.cloned.1.call-done = bf16[1536,1536]{1,0:T(8,128)(2,1)} async-done(((bf16[192,1536]{1,0:T(8,128)(2,1)}), bf16[1536,1536]{1,0:T(8,128)(2,1)}) %all-gather.19.cloned.1.call-update) | async-done | bytes 4718608 | tf_op jit(solution)/shard_map/all_gather | solution.py:132
  184.8 6.6 copy.108
  191.4 3.5 multiply_reduce_fusion.5
  196.4 40.2 %all-gather.17.cloned.1.call-done = bf16[2,1024,512]{1,2,0:T(8,128)(2,1)} async-done(((bf16[2,128,512]{1,2,0:T(8,128)(2,1)}), bf16[2,1024,512]{1,2,0:T(8,128)(2,1)}) %all-gather.17.cloned.1.call-update) | async-done | bytes 2097168 | tf_op jit(solution)/shard_map/all_gather | solution.py:161
  236.5 51.8 %all-gather.13.cloned.1.call-done = bf16[2,1024,512]{1,2,0:T(8,128)(2,1)} async-done(((bf16[2,128,512]{1,2,0:T(8,128)(2,1)}), bf16[2,1024,512]{1,2,0:T(8,128)(2,1)}) %all-gather.13.cloned.1.call-update) | async-done | bytes 2097168 | tf_op jit(solution)/shard_map/all_gather | solution.py:162
  288.3 35.3 %while.34 = (s32[]{:T(128)}, bf16[2,128,8,3,64]{1,4,3,0,2:T(8,128)(2,1)S(1)}, f32[8,2,3,128]{3,2,1,0:T(4,128)S(1)}, bf16[2,1024,512]{1,2,0:T(8,128)(2,1)}, bf16[...) while((s32[]{:T(128)}, ...), condition=%wide.region_6.7_spmd.clone, body=%wide.region_3.6_spmd.clone.sunk | while | flops 210894080 | bytes 10812071 | solution.py:194
  324.5 44.5 %all-gather.21.cloned.1.call-done = bf16[1536,1536]{1,0:T(8,128)(2,1)} async-done(((bf16[192,1536]{1,0:T(8,128)(2,1)}), bf16[1536,1536]{1,0:T(8,128)(2,1)}) %all-gather.21.cloned.1.call-update) | async-done | bytes 4718608 | tf_op jit(solution)/shard_map/all_gather | solution.py:135
  369.0 3.8 multiply_reduce_fusion.4
  374.2 401.8 %all-gather.23.cloned.1.call-done = bf16[1536,6912]{1,0:T(8,128)(2,1)} async-done(((bf16[192,6912]{1,0:T(8,128)(2,1)}), bf16[1536,6912]{1,0:T(8,128)(2,1)}) %all-gather.23.cloned.1.call-update) | async-done | bytes 21233680 | tf_op jit(solution)/shard_map/all_gather | solution.py:139
  776.0 14.7 fusion.118
  790.7 394.1 %all-gather.25.cloned.1.call-done = bf16[1536,6912]{1,0:T(8,128)(2,1)} async-done(((bf16[192,6912]{1,0:T(8,128)(2,1)}), bf16[1536,6912]{1,0:T(8,128)(2,1)}) %all-gather.25.cloned.1.call-update) | async-done | bytes 21233680 | tf_op jit(solution)/shard_map/all_gather | solution.py:140
  1184.8 14.7 fusion.119
  1199.5 394.1 %all-gather.27.cloned.1.call-done = bf16[6912,1536]{1,0:T(8,128)(2,1)} async-done(((bf16[864,1536]{1,0:T(8,128)(2,1)}), bf16[6912,1536]{1,0:T(8,128)(2,1)}) %all-gather.27.cloned.1.call-update) | async-done | bytes 21233680 | tf_op jit(solution)/shard_map/all_gather | solution.py:141
  1593.6 24.7 multiply_convert_fusion
  1618.3 11.1 fusion.120
  1629.4 12.0 multiply_reduce_fusion
  1643.5 5.2 convolution_convert_fusion.6
  1656.9 77.6 %while.35 = (s32[]{:T(128)}, f32[2,128,8,3,64]{1,4,3,2,0:T(8,128)}, bf16[2,1024,512]{1,2,0:T(8,128)(2,1)}, bf16[2,1024,512]{1,2,0:T(8,128)(2,1)}, bf16[2,1024,51...) while((s32[]{:T(128)}, f32[2,128,8,3,64]{1,4,3,2,0:T(8,128)}, ...), condition=%wide.region_11.12_spmd.clone, body=%wide.region_9.11_spmd.clone.sunk | while | flops 510704896 | bytes 26495184 | solution.py:291
  1734.5 6.2 copy.132
  1744.2 3.9 copy.117
  1748.3 64.0 %reduce-scatter.29.cloned.1.call-done = bf16[128,1024]{1,0:T(8,128)(2,1)} async-done(((bf16[1024,1024]{1,0:T(8,128)(2,1)}), bf16[128,1024]{1,0:T(8,128)(2,1)}) %reduce-scatter.29.cloned.1.call-update) | async-done | bytes 262160
  1819.3 64.1 %reduce-scatter.13.cloned.1.call-done = bf16[2,128,512]{2,1,0:T(8,128)(2,1)} async-done(((bf16[2,1024,512]{2,1,0:T(8,128)(2,1)}), bf16[2,128,512]{2,1,0:T(8,128)(2,1)}) %reduce-scatter.13.cloned.1.call-update) | async-done | bytes 262160 | tf_op jit(solution)/shard_map/reduce_scatter | solution.py:305
  1886.1 4.7 convolution_convert_fusion.3
  1895.8 3.6 convolution_convert_fusion.4
  1899.5 12.4 convolution_convert_fusion.2
  1912.0 12.3 convolution_convert_fusion.1
  1926.3 11.5 convolution_convert_fusion
  1939.7 3.8 fusion.76
  1943.4 7.0 reduce-scatter.17.cloned.1.call-done
  1950.4 68.1 %reduce-scatter.19.cloned.1.call-done = bf16[192,512]{1,0:T(8,128)(2,1)} async-done(((bf16[1536,512]{1,0:T(8,128)(2,1)}), bf16[192,512]{1,0:T(8,128)(2,1)}) %reduce-scatter.19.cloned.1.call-update) | async-done | bytes 196624 | tf_op jit(solution)/shard_map/reduce_scatter | solution.py:340
  2018.6 98.5 %reduce-scatter.21.cloned.1.call-done = bf16[192,1536]{1,0:T(8,128)(2,1)} async-done(((bf16[1536,1536]{1,0:T(8,128)(2,1)}), bf16[192,1536]{1,0:T(8,128)(2,1)}) %reduce-scatter.21.cloned.1.call-update) | async-done | bytes 589840 | tf_op jit(solution)/shard_map/reduce_scatter | solution.py:343
  2117.0 99.1 %reduce-scatter.15.cloned.1.call-done = bf16[192,1536]{1,0:T(8,128)(2,1)} async-done(((bf16[1536,1536]{1,0:T(8,128)(2,1)}), bf16[192,1536]{1,0:T(8,128)(2,1)}) %reduce-scatter.15.cloned.1.call-update) | async-done | bytes 589840 | tf_op jit(solution)/shard_map/reduce_scatter | solution.py:334
  2216.1 350.2 %reduce-scatter.23.cloned.1.call-done = bf16[192,6912]{1,0:T(8,128)(2,1)} async-done(((bf16[1536,6912]{1,0:T(8,128)(2,1)}), bf16[192,6912]{1,0:T(8,128)(2,1)}) %reduce-scatter.23.cloned.1.call-update) | async-done | bytes 2654224 | tf_op jit(solution)/shard_map/reduce_scatter | solution.py:229
  2566.3 350.1 %reduce-scatter.25.cloned.1.call-done = bf16[192,6912]{1,0:T(8,128)(2,1)} async-done(((bf16[1536,6912]{1,0:T(8,128)(2,1)}), bf16[192,6912]{1,0:T(8,128)(2,1)}) %reduce-scatter.25.cloned.1.call-update) | async-done | bytes 2654224 | tf_op jit(solution)/shard_map/reduce_scatter | solution.py:235
  2916.4 350.2 %reduce-scatter.27.cloned.1.call-done = bf16[864,1536]{1,0:T(8,128)(2,1)} async-done(((bf16[6912,1536]{1,0:T(8,128)(2,1)}), bf16[864,1536]{1,0:T(8,128)(2,1)}) %reduce-scatter.27.cloned.1.call-update) | async-done | bytes 2654224 | tf_op jit(solution)/shard_map/reduce_scatter | solution.py:223
  3268.0 13.0 fusion.59
  3284.7 18.9 all-reduce
  3303.6 6.5 psum.63
  3313.8 129.6 %all-reduce.4.cloned.1.call-done = (bf16[192,1536]{1,0:T(8,128)(2,1)}, bf16[192,512]{1,0:T(8,128)(2,1)}, bf16[192,512]{1,0:T(8,128)(2,1)}, bf16[192,1536]{1,0:T(...) async-done(((bf16[192,1536]{1,0:T(8,128)(2,1)}, bf16[192,512]{1,0:T(8,128)(2,1)}, bf16[192,512]{1,0:T(8,128)(2,1)}, ...) | async-done | bytes 9535504 | tf_op jit(solution)/shard_map/psum | solution.py:351
  3443.4 13.2 multiply_subtract_fusion
  3458.5 22.3 multiply_subtract_fusion.1
  3484.3 6.2 multiply_subtract_fusion.3
  (348 shorter events, 178.9 us)
Async XLA Ops:
  7.2 27.9 copy-start
  7.2 50.3 %all-gather.15.cloned.1.call-start = ((), (), s32[]{:S(2)}) async-start(), calls=%async_computation.11 | async-start | bytes 1769472 | tf_op jit(solution)/shard_map/all_gather | solution.py:133
  9.1 94.2 %all-gather.11.cloned.1.call-start = ((), (), s32[]{:S(2)}) async-start(), calls=%async_computation.9 | async-start | bytes 1769472 | tf_op jit(solution)/shard_map/all_gather | solution.py:134
  10.9 173.9 %all-gather.19.cloned.1.call-start = ((), (), s32[]{:S(2)}) async-start(), calls=%async_computation.13 | async-start | bytes 5308416 | tf_op jit(solution)/shard_map/all_gather | solution.py:132
  11.9 224.7 %all-gather.17.cloned.1.call-start = ((), (), s32[]{:S(2)}) async-start(), calls=%async_computation.12 | async-start | bytes 2359296 | tf_op jit(solution)/shard_map/all_gather | solution.py:161
  35.1 24.1 copy-start.37
  35.9 24.6 copy-start.49
  36.6 24.2 copy-start.32
  36.7 159.3 %copy-start.30 = (f32[128,32]{0,1:T(8,128)}, f32[128,32]{0,1:T(8,128)S(1)}, u32[]{:S(2)}) copy-start(f32[128,32]{0,1:T(8,128)S(1)} %get-tuple-element.505) | copy-start | bytes 49156
  36.9 154.5 %copy-start.2 = (bf16[2,128,1536]{2,1,0:T(8,128)(2,1)}, bf16[2,128,1536]{2,1,0:T(8,128)(2,1)S(1)}, u32[]{:S(2)}) copy-start(bf16[2,128,1536]{2,1,0:T(8,128)(2,1)S(1)} %fusion.62) | copy-start | bytes 2359300
  61.7 226.6 %all-gather.13.cloned.1.call-start = ((), (), s32[]{:S(2)}) async-start(), calls=%async_computation.10 | async-start | bytes 2359296 | tf_op jit(solution)/shard_map/all_gather | solution.py:162
  62.0 45.9 %copy-start.17 = (f32[192,1536]{1,0:T(8,128)S(1)}, f32[192,1536]{1,0:T(8,128)}, u32[]{:S(2)}) copy-start(f32[192,1536]{1,0:T(8,128)} %param.35) | copy-start | bytes 3538948
  107.8 261.2 %all-gather.21.cloned.1.call-start = ((), (), s32[]{:S(2)}) async-start(), calls=%async_computation.14 | async-start | bytes 5308416 | tf_op jit(solution)/shard_map/all_gather | solution.py:135
  108.8 667.2 %all-gather.23.cloned.1.call-start = ((), (), s32[]{:S(2)}) async-start(), calls=%async_computation.15 | async-start | bytes 23887872 | tf_op jit(solution)/shard_map/all_gather | solution.py:139
  113.1 1071.7 %all-gather.25.cloned.1.call-start = ((), (), s32[]{:S(2)}) async-start(), calls=%async_computation.16 | async-start | bytes 23887872 | tf_op jit(solution)/shard_map/all_gather | solution.py:140
  117.7 1476.0 %all-gather.27.cloned.1.call-start = ((), (), s32[]{:S(2)}) async-start(), calls=%async_computation.17 | async-start | bytes 23887872 | tf_op jit(solution)/shard_map/all_gather | solution.py:141
  122.1 1690.2 %reduce-scatter.29.cloned.1.call-start = ((), (), s32[]{:S(2)}) async-start(), calls=%async_computation.26 | async-start | bytes 2359296
  324.5 48.4 %copy-start.13 = (bf16[2,128,8,3,64]{1,0,4,3,2:T(2,128)(2,1)}, bf16[2,128,8,3,64]{1,0,4,3,2:T(2,128)(2,1)S(1)}, u32[]{:S(2)}) copy-start(bf16[2,128,8,3,64]{1,0,4,3,2:T(2,128)(2,1)S(1)} %copy.111) | copy-start | bytes 2359300
  369.0 5.0 copy-start.43
  790.7 802.9 %copy-start.21 = (bf16[2,128,1536]{2,1,0:T(8,128)(2,1)S(1)}, bf16[2,128,1536]{2,1,0:T(8,128)(2,1)}, u32[]{:S(2)}) copy-start(bf16[2,128,1536]{2,1,0:T(8,128)(2,1)} %param.31) | copy-start | bytes 2359300
  1618.3 11.1 copy-start.10
  1643.5 242.6 %copy-start.6 = (f32[256,1536]{1,0:T(8,128)}, f32[256,1536]{1,0:T(8,128)S(1)}, u32[]{:S(2)}) copy-start(f32[256,1536]{1,0:T(8,128)S(1)} %subtract_add_fusion) | copy-start | bytes 4718596
  1744.2 139.1 %reduce-scatter.13.cloned.1.call-start = ((), (), s32[]{:S(2)}) async-start(), calls=%async_computation.18 | async-start | bytes 2359296 | tf_op jit(solution)/shard_map/reduce_scatter | solution.py:305
  1748.2 65.5 %copy-start.31 = (f32[128,32]{0,1:T(8,128)S(1)}, f32[128,32]{0,1:T(8,128)}, u32[]{:S(2)}) copy-start(f32[128,32]{0,1:T(8,128)} %copy-done.30) | copy-start | bytes 49156
  1748.2 65.5 %copy-start.34 = (f32[128,32]{0,1:T(8,128)S(1)}, f32[128,32]{0,1:T(8,128)}, u32[]{:S(2)}) copy-start(f32[128,32]{0,1:T(8,128)} %copy-done.32) | copy-start | bytes 49156
  1748.2 65.6 %copy-start.41 = (f32[2,128,8]{1,2,0:T(8,128)S(1)}, f32[2,128,8]{1,2,0:T(8,128)}, u32[]{:S(2)}) copy-start(f32[2,128,8]{1,2,0:T(8,128)} %copy-done.40) | copy-start | bytes 24580
  1748.2 65.6 %copy-start.50 = (f32[64]{0:T(128)S(1)}, f32[64]{0:T(128)}, u32[]{:S(2)}) copy-start(f32[64]{0:T(128)} %copy-done.49) | copy-start | bytes 772
  1748.2 67.0 %copy-start.44 = (f32[2,128,8]{1,2,0:T(8,128)S(1)}, f32[2,128,8]{1,2,0:T(8,128)}, u32[]{:S(2)}) copy-start(f32[2,128,8]{1,2,0:T(8,128)} %get-tuple-element.501) | copy-start | bytes 24580
  1748.2 202.2 %reduce-scatter.17.cloned.1.call-start = ((), (), s32[]{:S(2)}) async-start(), calls=%async_computation.20 | async-start | bytes 1769472 | tf_op jit(solution)/shard_map/reduce_scatter | solution.py:337
  1819.2 199.3 %reduce-scatter.19.cloned.1.call-start = ((), (), s32[]{:S(2)}) async-start(), calls=%async_computation.21 | async-start | bytes 1769472 | tf_op jit(solution)/shard_map/reduce_scatter | solution.py:340
  1886.0 231.0 %reduce-scatter.21.cloned.1.call-start = ((), (), s32[]{:S(2)}) async-start(), calls=%async_computation.22 | async-start | bytes 5308416 | tf_op jit(solution)/shard_map/reduce_scatter | solution.py:343
  1890.9 325.3 %reduce-scatter.15.cloned.1.call-start = ((), (), s32[]{:S(2)}) async-start(), calls=%async_computation.19 | async-start | bytes 5308416 | tf_op jit(solution)/shard_map/reduce_scatter | solution.py:334
  1899.4 666.9 %reduce-scatter.23.cloned.1.call-start = ((), (), s32[]{:S(2)}) async-start(), calls=%async_computation.23 | async-start | bytes 23887872 | tf_op jit(solution)/shard_map/reduce_scatter | solution.py:229
  1911.9 1004.5 %reduce-scatter.25.cloned.1.call-start = ((), (), s32[]{:S(2)}) async-start(), calls=%async_computation.24 | async-start | bytes 23887872 | tf_op jit(solution)/shard_map/reduce_scatter | solution.py:235
  1924.3 1342.3 %reduce-scatter.27.cloned.1.call-start = ((), (), s32[]{:S(2)}) async-start(), calls=%async_computation.25 | async-start | bytes 23887872 | tf_op jit(solution)/shard_map/reduce_scatter | solution.py:223
  1937.8 1505.6 %all-reduce.4.cloned.1.call-start = ((), (), s32[]{:S(2)}) async-start(), calls=%async_computation.27 | async-start | bytes 19070976 | tf_op jit(solution)/shard_map/psum | solution.py:351
  3268.0 13.0 copy-start.8
  3268.0 13.0 copy-start.23
  3282.7 27.5 copy-start.52
  3282.7 27.5 copy-start.55
  3282.7 27.5 copy-start.56
  3282.7 28.1 copy-start.7
  3443.4 13.2 slice-start
  3443.4 14.6 slice-start.2
  3443.4 14.8 slice-start.1
  3443.4 15.1 slice-start.3
  3458.5 22.3 copy-start.24
  3458.5 22.3 copy-start.25
  (33 other events, 65.2 us)
Sparse Core Ops, SparseCore 0:
  10.8 46.6 all-gather.14
  60.3 42.9 all-gather.10
  106.1 78.6 all-gather.18
  187.3 49.1 all-gather.16
  239.0 49.2 all-gather.12
  290.9 78.0 all-gather.20
  371.1 404.8 all-gather.22
  778.1 406.6 all-gather.24
  1186.9 406.6 all-gather.26
  1744.3 67.9 reduce-scatter.28
  1816.4 66.8 reduce-scatter.12
  1886.6 63.7 reduce-scatter.16
  1954.8 63.7 reduce-scatter.18
  2022.6 94.3 reduce-scatter.20
  2121.1 94.9 reduce-scatter.14
  2219.9 346.3 reduce-scatter.22
  2570.5 345.8 reduce-scatter.24
  2920.2 346.3 reduce-scatter.26
  3270.2 173.1 all-reduce.3
where the time goes:
time: 3500 us
  waiting for transfers between devices  3030 us (87%)
  matrix products  256 us (7%)
  other arithmetic  88.9 us (3%)
  local copies, waits for them, and re-layouts  55 us (2%)
  blocking collectives  47.8 us (1%)
    all_gather x1, waiting for transfers between devices, body(): lax.all_gather(gate_shard, 'ctx', axis=0, tiled=True)  402 us
    all_gather x1, waiting for transfers between devices, body(): lax.all_gather(up_shard, 'ctx', axis=0, tiled=True)  394 us
    all_gather x1, waiting for transfers between devices, body(): lax.all_gather(down_shard, 'ctx', axis=0, tiled=True)  394 us
    reduce_scatter x1, waiting for transfers between devices, body(): lax.psum_scatter(product_rows(normed_two, gate_grad_low).astype(jnp.bfloa...  350 us
    reduce_scatter x1, waiting for transfers between devices, body(): lax.psum_scatter(product_rows(hidden_low, grad_low).astype(jnp.bfloat16),...  350 us
    reduce_scatter x1, waiting for transfers between devices, body(): lax.psum_scatter(product_rows(normed_two, up_grad_low).astype(jnp.bfloat1...  350 us
    psum x1, waiting for transfers between devices, body(): lax.psum(query_part.astype(jnp.bfloat16), 'rep').astype(jnp.float32)  130 us
    reduce_scatter x1, waiting for transfers between devices, body(): lax.psum_scatter(query_term.astype(jnp.bfloat16), 'ctx', scatter_dimensio...  99.1 us
  transfers between devices with their start and end apart: 19, of which 19 were waited for; matrix products, arithmetic and copies ran while one was open for 6% of the time, Pallas kernels for 0%

commit v1 on v0

v1 whole, which is shorter than its diff:
```python
import functools

import jax
import jax.numpy as jnp
import numpy as np
from jax import lax
from jax.experimental import pallas as pl
from jax.experimental.pallas import tpu as pltpu
from jax.sharding import PartitionSpec as P

MESH = pl.DeviceIdType.MESH
ANY = pl.BlockSpec(memory_space=pltpu.HBM)
VMEM = pl.BlockSpec(memory_space=pltpu.VMEM)
VMEM_BYTES = 60 * 1024 * 1024

HD = 64
STEP = 5


norm_eps = 1e-05
rope_base = 1000000.0
score_scale = 0.125
beta_one = 0.9
beta_two = 0.95
adam_eps = 1e-08


def product(left, right):
    return jnp.dot(left, right, preferred_element_type=jnp.float32)


def product_back(left, right):
    return lax.dot_general(
        left, right, (((1,), (1,)), ((), ())), preferred_element_type=jnp.float32
    )


def product_rows(left, right):
    return lax.dot_general(
        left, right, (((0,), (0,)), ((), ())), preferred_element_type=jnp.float32
    )


def rms_scale(values):
    return lax.rsqrt(jnp.mean(values * values, axis=-1, keepdims=True) + norm_eps)


def norm_back(grad, values, gain):
    scale = rms_scale(values)
    scaled = grad * gain
    inner = jnp.mean(scaled * values, axis=-1, keepdims=True)
    return (scale * scaled - values * (scale * scale * scale) * inner, grad * values * scale)


def rotary_tables(start, count, head_dim):
    half = head_dim // 2
    inverse = jnp.power(
        jnp.float32(rope_base), -(jnp.arange(half).astype(jnp.float32) * 2.0) / head_dim
    )
    angle = (start + jnp.arange(count)).astype(jnp.float32)[:, None] * inverse[None, :]
    return (jnp.cos(angle), jnp.sin(angle))


def rotary_constants(count, head_dim, seqs):
    half = head_dim // 2
    inverse = np.float32(rope_base) ** -(np.arange(half).astype(np.float32) * np.float32(2.0) / np.float32(head_dim))
    angle = np.arange(count).astype(np.float32)[:, None] * inverse.astype(np.float32)[None, :]
    cosine, sine = np.cos(angle), np.sin(angle)
    return (
        np.concatenate([cosine, cosine] * seqs, axis=1).astype(np.float32),
        np.concatenate([-sine, sine] * seqs, axis=1).astype(np.float32),
    )


def rotate(values, cosine, sine):
    half = values.shape[-1] // 2
    first = values[..., :half]
    second = values[..., half:]
    cosine = cosine[:, None, :]
    sine = sine[:, None, :]
    return jnp.concatenate(
        [first * cosine - second * sine, second * cosine + first * sine], axis=-1
    )


def rotate_back(grads, cosine, sine):
    half = grads.shape[-1] // 2
    first = grads[..., :half]
    second = grads[..., half:]
    cosine = cosine[:, None, :]
    sine = sine[:, None, :]
    return jnp.concatenate(
        [first * cosine + second * sine, second * cosine - first * sine], axis=-1
    )


def adamw(weight, grad, first, second, rate, decay):
    first_new = beta_one * first + (1.0 - beta_one) * grad
    second_new = beta_two * second + (1.0 - beta_two) * grad * grad
    fix_one = 1.0 - beta_one**STEP
    fix_two = 1.0 - beta_two**STEP
    update = first_new / fix_one / (jnp.sqrt(second_new / fix_two) + adam_eps)
    return (weight - rate * (update + decay * weight), first_new, second_new)


def swap(blocks):
    return lax.all_to_all(blocks, "ctx", 0, 0)


def gather(block):
    return lax.all_gather(block, "ctx", axis=0, tiled=False)


def scatter_sum(blocks):
    return lax.psum_scatter(blocks, "ctx", scatter_dimension=0, tiled=False)


def rep_sum(values):
    return lax.psum(values, "rep")


def rep_pairs(bit):
    return [(i, i ^ bit) for i in range(lax.axis_size("rep"))]


def rep_fold(total, bit):
    low = jnp.bfloat16
    mine = (lax.axis_index("rep") // bit) % 2
    pairs = total.reshape((total.shape[0] // 2, 2) + total.shape[1:])
    keep = lax.dynamic_index_in_dim(pairs, mine, 1, keepdims=False)
    give = lax.dynamic_index_in_dim(pairs, 1 - mine, 1, keepdims=False).astype(low)
    got = lax.ppermute(give, "rep", rep_pairs(bit))
    return keep.astype(jnp.float32) + got.astype(jnp.float32)


def rep_scatter(total, bit=1):
    while total.shape[0] > 1:
        total = rep_fold(total, bit)
        bit *= 2
    return total[0].astype(jnp.bfloat16)


def rep_gather(block):
    whole = block[None]
    bit = lax.axis_size("rep") // 2
    while bit > 0:
        mine = (lax.axis_index("rep") // bit) % 2
        got = lax.ppermute(whole, "rep", rep_pairs(bit))
        first = jnp.where(mine == 0, whole, got)
        second = jnp.where(mine == 0, got, whole)
        whole = jnp.stack([first, second], axis=1).reshape((-1,) + block.shape)
        bit //= 2
    return whole


def ring_place(index, n):
    deep = lax.div(index, 2)
    side = lax.rem(index, 2)
    return deep + side * (n - 1 - 2 * deep)


def ring_index(place, n):
    side = lax.div(place, n // 2)
    deep = place + side * (n - 1 - 2 * place)
    return 2 * deep + side


def around(place, hops, n):
    return ring_index(lax.rem(place + hops + 2 * n, n), n)


def greet(others, partners=()):
    barrier = pltpu.get_barrier_semaphore()
    for other in others:
        pl.semaphore_signal(barrier, inc=1, device_id={"ctx": other}, device_id_type=MESH)
    for other in partners:
        pl.semaphore_signal(barrier, inc=1, device_id={"rep": other}, device_id_type=MESH)
    pl.semaphore_wait(barrier, len(others) + len(partners))


def remote(source, target, send, recv, other, axis="ctx"):
    return pltpu.make_async_remote_copy(
        src_ref=source,
        dst_ref=target,
        send_sem=send,
        recv_sem=recv,
        device_id={axis: other},
        device_id_type=MESH,
    )


def rep_partners():
    place = lax.axis_index("rep")
    return place + 1 - 2 * lax.rem(place, 2), lax.rem(place + 2, 4)


class RepShare:
    def __init__(self, pieces, send, recv, own_sem):
        self.pieces, self.send, self.recv, self.own_sem = pieces, send, recv, own_sem
        self.core, self.across = rep_partners()
        self.place = lax.axis_index("rep")
        self.beyond = lax.rem(self.core + 2, 4)

    def copy(self, at, which):
        source, target = self.pieces[at]
        there = target(self.across if which == 2 else self.place)
        return remote(
            there if which == 2 else source,
            there,
            self.send.at[at, which],
            self.recv.at[at, which],
            self.across if which == 0 else self.core,
            "rep",
        )

    def own(self, at):
        source, target = self.pieces[at]
        return pltpu.make_async_copy(source, target(self.place), self.own_sem.at[at])

    def arrival(self, at, which):
        _, target = self.pieces[at]
        there = target((self.across, self.core, self.beyond)[which])
        return remote(
            there, there, self.send.at[at, which], self.recv.at[at, which], self.core, "rep"
        )

    def begin(self):
        for at in range(len(self.pieces)):
            self.copy(at, 0).start()
            self.copy(at, 1).start()
            self.own(at).start()

    def middle(self, only=None):
        for at in range(len(self.pieces)) if only is None else (only,):
            self.arrival(at, 0).wait_recv()
            self.copy(at, 2).start()

    def end(self):
        for at in range(len(self.pieces)):
            self.own(at).wait()
            for which in range(3):
                if which > 0:
                    self.arrival(at, which).wait_recv()
                self.copy(at, which).wait_send()


def add_into(total, other, step):
    @pl.loop(0, total.shape[0] // step)
    def _(at):
        here = pl.ds(pl.multiple_of(at * step, step), step)
        summed = total[here].astype(jnp.float32) + other[here].astype(jnp.float32)
        total[here] = summed.astype(total.dtype)


def add_columns(total, other, step):
    @pl.loop(0, total.shape[1] // step)
    def _(at):
        here = pl.ds(pl.multiple_of(at * step, step), step)
        summed = total[:, here].astype(jnp.float32) + other[:, here].astype(jnp.float32)
        total[:, here] = summed.astype(total.dtype)


def entry_kernel(n, head_dim, x_ref, g_ref, wq_ref, wk_ref, wv_ref, wo_ref, wg_ref, wu_ref, *refs):
    wd_ref, h_out, lin_out, g_out, o_out, q_out, wg_out, wu_out, wd_out = refs[:9]
    x_all, h_all, w_all, gain, mixed, q_own, o_own, f_own = refs[9:17]
    wq, wk, wv, wo, wf, wd, f_all, wd_low = refs[17:25]
    x_send, x_recv, p_send, p_recv, own_sem, load_sem, h_sem, r_send, r_recv, r_own = refs[25:]
    f32, low = jnp.float32, jnp.bfloat16
    me = lax.axis_index("ctx")
    place = ring_place(me, n)
    others = [lax.rem(me + hop, n) for hop in range(1, n)]
    right, left = around(place, 1, n), around(place, -1, n)
    quarter = x_ref.shape[0] // 4
    span = x_ref.shape[0] // 2
    width = x_ref.shape[1]
    share = o_own.shape[0]
    rep_rows = pl.ds(pl.multiple_of(lax.axis_index("rep") * share, 16), share)
    loads = [
        pltpu.make_async_copy(source, target, load_sem.at[at])
        for at, (source, target) in enumerate(
            (
                (wq_ref, wq),
                (wk_ref, wk),
                (wv_ref, wv),
                (wo_ref.at[rep_rows], wo),
                (wg_ref.at[rep_rows], wf.at[0]),
                (wu_ref.at[rep_rows], wf.at[1]),
                (wd_ref, wd),
            )
        )
    ]
    for at in (4, 5, 0, 1, 2, 3, 6):
        loads[at].start()
    pieces = [(x_ref, x_all, (pl.ds(part * quarter, quarter),), part < 2) for part in (0, 2, 1, 3)]
    for source, target in ((o_own, o_out), (q_own, q_out)):
        wide = source.shape[1] // 2
        pieces += [
            (source, target, (slice(None), pl.ds(part * wide, wide)), part < 1) for part in (0, 1)
        ]
    tokens, weights = range(4), range(4, len(pieces))

    def owner_of(step, up):
        return around(place, -1 - step if up else 1 + step, n)

    def hop_copy(at, step):
        source, target, where, up = pieces[at]
        owner = owner_of(step, up)
        first = isinstance(step, int) and step < 0
        return remote(
            source.at[where] if first else target.at[(owner,) + where],
            target.at[(owner,) + where],
            x_send.at[at, step + 1],
            x_recv.at[at, step + 1],
            right if up else left,
        )

    def arrived(at, step):
        _, target, where, up = pieces[at]
        block = target.at[(owner_of(step, up),) + where]
        remote(block, block, x_send.at[at, step], x_recv.at[at, step], right).wait_recv()

    def pass_first(step):
        for at in range(len(pieces)):
            arrived(at, step)
            hop_copy(at, step).start()

    def pass_on(which, step):
        @pl.when(step < n - 1)
        def _():
            for at in which:
                arrived(at, step)

                @pl.when(step < n - 2)
                def _():
                    hop_copy(at, step).start()

    def swap_copy(at, hop):
        other = others[hop - 1]
        source, target = (
            (mixed.at[other], w_all.at[me]),
            (g_ref, g_out.at[me]),
            (f_own.at[other], f_all.at[:, me]),
        )[at]
        return remote(source, target, p_send.at[at, hop], p_recv.at[at, hop], other)

    own = [
        pltpu.make_async_copy(source, target, own_sem.at[at])
        for at, (source, target) in enumerate(
            (
                (x_ref, x_all.at[me]),
                (g_ref, g_out.at[me]),
                (mixed.at[me], w_all.at[me]),
                (o_own, o_out.at[me]),
                (q_own, q_out.at[me]),
                (f_own.at[me], f_all.at[:, me]),
            )
        )
    ]
    share_feed = RepShare(
        [
            (f_all.at[0], lambda r: wg_out.at[:, r]),
            (f_all.at[1], lambda r: wu_out.at[:, r]),
        ],
        r_send,
        r_recv,
        r_own,
    )
    own[0].start()
    own[1].start()
    greet(others, rep_partners())
    for at in tokens:
        hop_copy(at, -1).start()
    for copy in loads[4:6]:
        copy.wait()
    wide = f_own.shape[3]
    for owner in range(n):
        for at in (0, 1):
            f_own[owner, at] = wf[at, :, owner * wide : (owner + 1) * wide].astype(low)
    own[5].start()
    for hop in range(1, n):
        swap_copy(2, hop).start()
    for copy in loads[:3]:
        copy.wait()
    for source, at, wide in ((wq, 0, wq.shape[1] // n), (wk, 1, head_dim), (wv, 2, head_dim)):
        start = (0, wq.shape[1] // n, wq.shape[1] // n + head_dim)[at]
        for owner in range(n):
            mixed[owner, :, start : start + wide] = source[
                :, owner * wide : (owner + 1) * wide
            ].astype(low)
    own[2].start()
    for hop in range(1, n):
        swap_copy(0, hop).start()
        swap_copy(1, hop).start()
    columns = mixed.shape[2]
    for owner in range(n):
        q_own[:, owner * columns : (owner + 1) * columns] = mixed[owner, rep_rows]
    loads[3].wait()
    o_own[...] = wo[...].astype(low)
    own[3].start()
    own[4].start()
    for at in weights:
        hop_copy(at, -1).start()
    pass_first(0)
    loads[6].wait()

    @pl.loop(0, wd.shape[0] // 16)
    def _(at):
        here = pl.ds(pl.multiple_of(at * 16, 16), 16)
        wd_low[here] = wd[here].astype(low)

    wd_give = pltpu.make_async_copy(wd_low, wd_out, own_sem.at[6])
    wd_give.start()
    for hop in range(1, n):
        swap_copy(0, hop).wait_recv()
        swap_copy(1, hop).wait_recv()
    for copy in own[:3]:
        copy.wait()
    few = gain.shape[1] // n
    for owner in range(n):
        gain[:, owner * few : (owner + 1) * few] = g_out[owner, :, :few]
    heads = lin_out.shape[0]

    def give_out(step, seq):
        owner = owner_of(step, seq == 0)
        return pltpu.make_async_copy(h_all.at[owner, seq], h_out.at[owner, seq], h_sem.at[seq, step])

    def multiply(step, seq):
        owner = owner_of(step, seq == 0)
        x = x_all[owner, pl.ds(seq * span, span)].astype(f32)
        normed = (x * rms_scale(x) * gain[0:1, :width]).astype(low)
        h_all[owner, seq] = normed
        give_out(step, seq).start()
        lin = product(normed, w_all[...].reshape(width, -1))
        rows = pl.ds(pl.multiple_of(owner * span, span), span)
        for head in range(heads):
            lin_out[head, rows, seq * head_dim : (seq + 1) * head_dim] = lin[
                :, head * head_dim : (head + 1) * head_dim
            ]

    multiply(n - 1, 0)
    multiply(n - 1, 1)

    @pl.loop(0, n - 1)
    def _(step):
        pass_on(tokens, step + 1)
        multiply(step, 0)
        pass_on(weights, step + 1)

        @pl.when(step == 2)
        def _():
            own[5].wait()
            for hop in range(1, n):
                swap_copy(2, hop).wait_recv()
            share_feed.begin()

        @pl.when(step == n - 2)
        def _():
            share_feed.middle()

        multiply(step, 1)

    wd_give.wait()
    for copy in own[3:5]:
        copy.wait()
    for at in range(len(pieces)):
        hop_copy(at, -1).wait_send()

        @pl.loop(0, n - 2)
        def _(step):
            hop_copy(at, step).wait_send()

    @pl.loop(0, n)
    def _(step):
        give_out(step, 0).wait()
        give_out(step, 1).wait()

    for hop in range(1, n):
        swap_copy(0, hop).wait_send()
        swap_copy(1, hop).wait_send()
        swap_copy(2, hop).wait_send()
    share_feed.end()


def enter(block, gains, shards, feed_shards, w_down, head_dim):
    n = lax.axis_size("ctx")
    rows, width = block.shape
    f32, low = jnp.float32, jnp.bfloat16
    shard, q_width = shards[0].shape
    kv_width = shards[1].shape[1]
    out_width = shards[3].shape[1]
    reps = lax.axis_size("rep")
    few = shard // reps
    all_width = q_width + 2 * kv_width
    feed_width = feed_shards[0].shape[1]
    return pl.pallas_call(
        functools.partial(entry_kernel, n, head_dim),
        out_shape=[
            jax.ShapeDtypeStruct((n, 2, rows // 2, width), low),
            jax.ShapeDtypeStruct((all_width // n // head_dim, n * rows // 2, 2 * head_dim), f32),
            jax.ShapeDtypeStruct((n,) + gains.shape, f32),
            jax.ShapeDtypeStruct((n, few, out_width), low),
            jax.ShapeDtypeStruct((n, few, all_width), low),
            jax.ShapeDtypeStruct((n, reps, few, feed_width // n), low),
            jax.ShapeDtypeStruct((n, reps, few, feed_width // n), low),
            jax.ShapeDtypeStruct(w_down.shape, low),
        ],
        in_specs=[ANY] * 9,
        out_specs=[ANY, VMEM, VMEM, ANY, ANY, ANY, ANY, ANY],
        scratch_shapes=[
            pltpu.VMEM((n, rows, width), low),
            pltpu.VMEM((n, 2, rows // 2, width), low),
            pltpu.VMEM((n, shard, all_width // n), low),
            pltpu.VMEM((gains.shape[0], width + head_dim), f32),
            pltpu.VMEM((n, shard, all_width // n), low),
            pltpu.VMEM((few, all_width), low),
            pltpu.VMEM((few, out_width), low),
            pltpu.VMEM((n, 2, few, feed_width // n), low),
            pltpu.VMEM((shard, q_width), f32),
            pltpu.VMEM((shard, kv_width), f32),
            pltpu.VMEM((shard, kv_width), f32),
            pltpu.VMEM((few, out_width), f32),
            pltpu.VMEM((2, few, feed_width), f32),
            pltpu.VMEM(w_down.shape, f32),
            pltpu.VMEM((2, n, few, feed_width // n), low),
            pltpu.VMEM(w_down.shape, low),
            pltpu.SemaphoreType.DMA((8, n)),
            pltpu.SemaphoreType.DMA((8, n)),
            pltpu.SemaphoreType.DMA((3, n)),
            pltpu.SemaphoreType.DMA((3, n)),
            pltpu.SemaphoreType.DMA((7,)),
            pltpu.SemaphoreType.DMA((7,)),
            pltpu.SemaphoreType.DMA((2, n)),
            pltpu.SemaphoreType.DMA((2, 3)),
            pltpu.SemaphoreType.DMA((2, 3)),
            pltpu.SemaphoreType.DMA((2,)),
        ],
        compiler_params=pltpu.CompilerParams(
            collective_id=0, has_side_effects=True, vmem_limit_bytes=VMEM_BYTES
        ),
    )(block, gains, *shards, *feed_shards, w_down)


def lane_half(shape):
    return lax.broadcasted_iota(jnp.int32, shape, len(shape) - 1) < shape[-1] // 2


def pack(first, second):
    return jnp.where(lane_half(first.shape), first, second)


def half_mean(values):
    left = lane_half(values.shape)
    one = jnp.sum(jnp.where(left, values, 0.0), axis=-1, keepdims=True)
    two = jnp.sum(jnp.where(left, 0.0, values), axis=-1, keepdims=True)
    return jnp.where(left, one, two) * (2.0 / values.shape[-1])


def half_turn(values):
    wide = values.shape[-1]
    lane = lax.broadcasted_iota(jnp.int32, values.shape, len(values.shape) - 1)
    axis = len(values.shape) - 1
    return jnp.where(
        lax.rem(lane, wide // 2) < wide // 4,
        pltpu.roll(values, wide - wide // 4, axis),
        pltpu.roll(values, wide // 4, axis),
    )


def side_by_side(blocks, flat):
    n, count, span, wide = blocks.shape
    half = wide // 2
    left = lane_half((span, wide))

    @pl.loop(0, n // 2)
    def _(pair):
        heads = [blocks[2 * pair + at, head].astype(jnp.float32) for at in (0, 1) for head in range(count)]
        for at in range(count):
            one, two = heads[2 * at], heads[2 * at + 1]
            cols = pl.ds(pl.multiple_of((pair * count + at) * wide, wide), wide)
            flat[0:span, cols] = jnp.where(left, one, pltpu.roll(two, half, 1)).astype(flat.dtype)
            flat[span : 2 * span, cols] = jnp.where(left, pltpu.roll(one, half, 1), two).astype(
                flat.dtype
            )


def masked(scores):
    block, keys = scores.shape
    row = lax.broadcasted_iota(jnp.int32, (block, block), 0)
    seen = lax.broadcasted_iota(jnp.int32, (block, block), 1) <= row
    last = jnp.where(seen, scores[:, keys - block :], -1e30)
    return last if keys == block else jnp.concatenate([scores[:, : keys - block], last], axis=1)


def scaled(queries):
    return (queries.astype(jnp.float32) * score_scale).astype(queries.dtype)


def halves(packed):
    left = lane_half(packed.shape)
    zero = jnp.zeros_like(packed)
    return jnp.where(left, packed, zero), jnp.where(left, zero, packed)


def attend_kernel(n, group, block, lin_ref, cos_ref, sin_ref, gain_ref, x_ref, norm_ref, *refs):
    dy_ref, wo_ref = refs[:2]
    low_give, lse_give, flat_out, resid_out, next_out, dy_give, wo_out = refs[2:9]
    o_own, o_out, w_all, low_out, lse_out, dy_out = refs[9:15]
    o_send, o_recv, dy_send, dy_recv, r_send, r_recv, r_own, own_sem = refs[15:]
    f32, low = jnp.float32, jnp.bfloat16
    me = lax.axis_index("ctx")
    place = ring_place(me, n)
    others = [lax.rem(me + hop, n) for hop in range(1, n)]
    toward = (around(place, 1, n), around(place, -1, n))
    length = lin_ref.shape[1]
    span = length // n
    rows = dy_ref.shape[0] // 2
    parts = (pl.ds(0, rows), pl.ds(rows, rows))
    share = RepShare(
        [(wo_ref, lambda r: wo_out.at[:, r])],
        r_send,
        r_recv,
        r_own,
    )
    greet(others, rep_partners())

    def ring(step, side):
        owner = around(place, -step if side == 0 else step, n)
        there = dy_out.at[owner, parts[side]]
        return remote(
            there, there, dy_send.at[side, step], dy_recv.at[side, step], toward[side]
        )

    def first(side):
        return remote(
            dy_ref.at[parts[side]],
            dy_out.at[me, parts[side]],
            dy_send.at[side, 0],
            dy_recv.at[side, 0],
            toward[side],
        )

    def hop_on(step):
        for side in (0, 1):
            owner = around(place, -1 - step if side == 0 else 1 + step, n)
            there = dy_out.at[owner, parts[side]]
            remote(
                there, there, dy_send.at[side, step], dy_recv.at[side, step], toward[side]
            ).wait_recv()

            @pl.when(step < n - 2)
            def _():
                ring(step + 1, side).start()

    def give(head, hop):
        return remote(
            o_own.at[head, pl.ds(pl.multiple_of(others[hop - 1] * span, span), span)],
            o_out.at[me, head],
            o_send.at[head, hop],
            o_recv.at[head, hop],
            others[hop - 1],
        )

    for side in (0, 1):
        first(side).start()
    share.begin()
    keep_dy = pltpu.make_async_copy(dy_ref, dy_out.at[me], own_sem.at[0])
    keep_dy.start()

    for head in range(group + 1):

        @pl.loop(0, length // block)
        def _(at):
            here = pl.ds(pl.multiple_of(at * block, block), block)
            u = lin_ref[head, here]
            gain = gain_ref[0:1] if head < group else gain_ref[1:2]
            z = u * lax.rsqrt(half_mean(u * u) + norm_eps) * gain
            low_out[head, here] = (z * cos_ref[here] + half_turn(z) * sin_ref[here]).astype(low)
            if head == group:
                low_out[group + 1, here] = lin_ref[group + 1, here].astype(low)

    @pl.loop(0, group)
    def _(head):
        for at in range(length // block):
            keys = (at + 1) * block
            here = pl.ds(at * block, block)
            outs, sums = [], []
            for query in halves(scaled(low_out[head, here])):
                scores = masked(product_back(query, low_out[group, :keys]))
                top = jnp.max(scores, axis=-1, keepdims=True)
                expo = jnp.exp(scores - top)
                total = jnp.sum(expo, axis=-1, keepdims=True)
                probs = (expo * (1.0 / total)).astype(low)
                outs.append(product(probs, low_out[group + 1, :keys]))
                sums.append(jnp.broadcast_to(top + jnp.log(total), (block, low_out.shape[2])))
            o_own[head, here] = pack(*outs).astype(low)
            lse_out[head, here] = pack(*sums)
            for unit in range(2, group * (length // block), 3):
                if unit % (length // block) == at:

                    @pl.when(head == unit // (length // block))
                    def _(unit=unit):
                        hop_on(unit // 3)

        for hop in range(1, n):
            give(head, hop).start()

    gives = [
        pltpu.make_async_copy(source, target, own_sem.at[3 + at])
        for at, (source, target) in enumerate(
            ((low_out, low_give), (lse_out, lse_give), (dy_out, dy_give))
        )
    ]
    gives[0].start()
    gives[1].start()
    served = group * (length // block) // 3
    middle = served + 1

    @pl.loop(served, middle)
    def _(step):
        hop_on(step)

    share.middle()

    @pl.loop(middle, n - 1)
    def _(step):
        hop_on(step)

    keep_dy.wait()
    gives[2].start()
    keep_o = pltpu.make_async_copy(
        o_own.at[:, pl.ds(pl.multiple_of(me * span, span), span)], o_out.at[me], own_sem.at[1]
    )
    keep_o.start()
    for side in (0, 1):
        first(side).wait_send()

        @pl.loop(1, n - 1)
        def _(step):
            ring(step, side).wait_send()

    @pl.loop(0, group)
    def _(head):
        for hop in range(1, n):
            give(head, hop).wait_send()
            source = lax.rem(me + n - hop, n)
            there = o_out.at[source, head]
            remote(
                there, there, o_send.at[head, hop], o_recv.at[head, hop], others[hop - 1]
            ).wait_recv()

    keep_o.wait()
    side_by_side(o_out, flat_out)
    share.end()
    fetch = pltpu.make_async_copy(wo_out, w_all, own_sem.at[2])
    fetch.start()
    fetch.wait()
    weights = w_all[...].reshape(-1, w_all.shape[3])
    x = x_ref[...].astype(f32)
    resid = x + product(flat_out[...], weights)
    resid_out[...] = resid
    next_out[...] = (resid * rms_scale(resid) * norm_ref[...]).astype(low)
    for copy in gives:
        copy.wait()


def attend(lin, cosine, sine, gain, tokens, norm_gain, grad, w_out):
    n = lax.axis_size("ctx")
    reps = lax.axis_size("rep")
    f32, low = jnp.float32, jnp.bfloat16
    count, length, wide = lin.shape
    group = count - 2
    return pl.pallas_call(
        functools.partial(attend_kernel, n, group, 256),
        out_shape=[
            jax.ShapeDtypeStruct((count, length, wide), low),
            jax.ShapeDtypeStruct((group, length, wide), f32),
            jax.ShapeDtypeStruct(tokens.shape, low),
            jax.ShapeDtypeStruct(tokens.shape, f32),
            jax.ShapeDtypeStruct(tokens.shape, low),
            jax.ShapeDtypeStruct((n,) + grad.shape, low),
            jax.ShapeDtypeStruct((n, reps) + w_out.shape[1:], low),
        ],
        in_specs=[VMEM] * 6 + [ANY] * 2,
        out_specs=[ANY] * 2 + [VMEM] * 3 + [ANY] * 2,
        scratch_shapes=[
            pltpu.VMEM((group, length, wide), low),
            pltpu.VMEM((n, group, length // n, wide), low),
            pltpu.VMEM((n, reps) + w_out.shape[1:], low),
            pltpu.VMEM((count, length, wide), low),
            pltpu.VMEM((group, length, wide), f32),
            pltpu.VMEM((n,) + grad.shape, low),
            pltpu.SemaphoreType.DMA((group, n)),
            pltpu.SemaphoreType.DMA((group, n)),
            pltpu.SemaphoreType.DMA((2, n)),
            pltpu.SemaphoreType.DMA((2, n)),
            pltpu.SemaphoreType.DMA((1, 3)),
            pltpu.SemaphoreType.DMA((1, 3)),
            pltpu.SemaphoreType.DMA((1,)),
            pltpu.SemaphoreType.DMA((6,)),
        ],
        compiler_params=pltpu.CompilerParams(
            collective_id=2, has_side_effects=True, vmem_limit_bytes=VMEM_BYTES
        ),
        cost_estimate=pl.CostEstimate(
            flops=16 * group * length * length * wide, bytes_accessed=2**26, transcendentals=0
        ),
    )(lin, cosine, sine, gain, tokens, norm_gain, grad, w_out)


def attend_back_kernel(n, group, block, low_src, lse_src, lin_src, cos_src, sin_src, gain_ref, b_ref, r_ref, dy_ref, *refs):
    f_ref, att_ref, wo_ref = refs[:3]
    g_keep, g_got, u_keep, u_got, d_keep, d_got, h_ref = refs[3:10]
    d_out, q_out, g_out, g_give, u_give, d_give, o_give, dr_out, f_out = refs[10:19]
    do_own, do_all, dk_sum, dv_sum, g1, g2, g3, u1, u2, u3, d1, d2, o_term, o2 = refs[19:33]
    d_own, g_swap, u_swap, h_all, q_term, q2, q_sum, g_flat, u_flat, d_sum, o_sum = refs[33:44]
    dr_low, low_ref, lse_ref, lin_ref, cos_ref, sin_ref = refs[44:50]
    do_send, do_recv, d_send, d_recv, own_sem, load_sem, x_send, x_recv = refs[50:58]
    a_send, a_recv, give_sem, head_sem = refs[58:]
    f32, low = jnp.float32, jnp.bfloat16
    me = lax.axis_index("ctx")
    others = [lax.rem(me + hop, n) for hop in range(1, n)]
    length, wide = lin_src.shape[1:]
    span = length // n

    def owned(index):
        return pl.ds(pl.multiple_of(index * span, span), span)

    def bring(head, hop):
        return remote(
            do_own.at[others[hop - 1], head],
            do_all.at[head, owned(me)],
            do_send.at[head, hop],
            do_recv.at[head, hop],
            others[hop - 1],
        )

    def give(head, hop):
        return remote(
            d_own.at[head, owned(others[hop - 1])],
            d_out.at[me, head],
            d_send.at[head, hop],
            d_recv.at[head, hop],
            others[hop - 1],
        )

    rep_place = lax.axis_index("rep")
    mine_core, mine_x = lax.rem(rep_place, 2), lax.div(rep_place, 2)
    core, across = rep_partners()
    loads = [
        pltpu.make_async_copy(source, target, load_sem.at[at])
        for at, (source, target) in enumerate(
            (
                (d_keep, d1),
                (d_got, d2),
                (g_keep, g1),
                (g_got, g2),
                (u_keep, u1),
                (u_got, u2),
                (wo_ref.at[pl.ds(0, n)], h_all.at[0]),
                (wo_ref.at[pl.ds(n, wo_ref.shape[0] - n)], h_all.at[1, pl.ds(0, wo_ref.shape[0] - n)]),
                (h_ref.at[:, 0], h_all.at[0]),
                (h_ref.at[:, 1], h_all.at[1]),
            )
        )
    ]
    head_loads = [
        pltpu.make_async_copy(source, target, head_sem.at[at])
        for at, (source, target) in enumerate(
            (
                (low_src, low_ref),
                (lse_src, lse_ref),
                (lin_src, lin_ref),
                (cos_src, cos_ref),
                (sin_src, sin_ref),
            )
        )
    ]
    for at in (6, 7, 2, 3, 4, 5, 0, 1):
        loads[at].start()
    for copy in head_loads:
        copy.start()

    def cross(at, source, target, other):
        return remote(source, target, x_send.at[at], x_recv.at[at], other, "rep")

    def crossing(at):
        if at == 5:
            return cross(5, q_term.at[:, :, 1 - mine_core], q2, core)
        if at == 4:
            return cross(4, o_term.at[:, :, 1 - mine_core], o2, core)
        if at == 0:
            return cross(0, d1.at[1 - mine_x], d_sum, across)
        source, target = ((g1, g3), (u1, u3), (o_term, o_sum))[at - 1]
        if at == 3:
            return cross(3, o_term.at[:, 1 - mine_x, mine_core], o_sum, across)
        return cross(at, source.at[:, 1 - mine_x], target, across)

    def swap_out(at, hop):
        source, target = ((g3, g_swap), (u3, u_swap))[at]
        other = others[hop - 1]
        return remote(
            source.at[other], target.at[me], a_send.at[at, hop], a_recv.at[at, hop], other
        )

    def swap_own(at):
        source, target = ((g3, g_swap), (u3, u_swap))[at]
        return pltpu.make_async_copy(source.at[me], target.at[me], own_sem.at[2 + at])

    greet(others, rep_partners())
    chunk = 64
    totals = jnp.zeros((1, f_ref.shape[1]), f32)
    for at in range(r_ref.shape[0] // chunk):
        here = pl.ds(at * chunk, chunk)
        back, terms = norm_back(b_ref[here].astype(f32), r_ref[here], f_ref[...])
        grads = dy_ref[here].astype(f32) + back
        totals += jnp.sum(terms, axis=0, keepdims=True)
        dr_out[here] = grads
        dr_low[here] = grads.astype(low)
    f_out[...] = jnp.broadcast_to(totals, f_out.shape)
    for copy in loads[6:8]:
        copy.wait()
    left = lane_half((span, wide))

    @pl.loop(0, n // 2)
    def _(pair):
        heads = []
        for at in range(group):
            index = pair * group + at
            both = product_back(dr_low[...], h_all[lax.div(index, n), lax.rem(index, n)])
            one, two = both[:span], both[span:]
            heads.append(jnp.where(left, one, pltpu.roll(two, wide // 2, 1)))
            heads.append(jnp.where(left, pltpu.roll(one, wide // 2, 1), two))
        for at, values in enumerate(heads):
            do_own[2 * pair + at // group, at % group] = values.astype(low)

    for copy in loads[8:]:
        copy.start()
    for head in range(group):
        for hop in range(1, n):
            bring(head, hop).start()
    keep_do = pltpu.make_async_copy(do_own.at[me], do_all.at[:, owned(me)], own_sem.at[0])
    keep_do.start()
    piece = d1.shape[1] // 6
    for copy in loads[2:4]:
        copy.wait()
    add_into(g1, g2, 1)
    crossing(1).start()
    for copy in loads[4:6]:
        copy.wait()
    add_into(u1, u2, 1)
    crossing(2).start()
    for copy in loads[:2]:
        copy.wait()
    add_columns(d1, d2, piece)
    crossing(0).start()
    shard = h_all.shape[3] // n

    @pl.loop(0, n // 2)
    def _(pair):
        cols = pl.ds(pl.multiple_of(pair * 2 * shard, 2 * shard), 2 * shard)
        part = product_rows(att_ref[:, cols], dr_low[...]).astype(low)
        o_term[pl.ds(2 * pair, 2)] = part.reshape(2, 2, 2, shard // 4, part.shape[1])

    crossing(4).start()
    dk_sum[...] = jnp.zeros_like(dk_sum)
    dv_sum[...] = jnp.zeros_like(dv_sum)
    g_out[...] = jnp.zeros_like(g_out)
    keep_do.wait()

    def head_back(grad, here, head, gain_at):
        turned = grad * cos_ref[here] - half_turn(grad) * sin_ref[here]
        u = lin_ref[head, here]
        scale = lax.rsqrt(half_mean(u * u) + norm_eps)
        scaled = turned * gain_ref[gain_at : gain_at + 1]
        inner = half_mean(scaled * u)
        g_out[gain_at : gain_at + 1] += jnp.sum(turned * u * scale, axis=0, keepdims=True)
        d_own[head, here] = (scale * scaled - u * (scale * scale * scale) * inner).astype(low)

    def swap_rows(at):
        first, total = ((g1, g3), (u1, u3))[at]
        crossing(1 + at).wait_recv()

        @pl.loop(0, n)
        def _(owner):
            summed = total[owner].astype(f32) + first[owner, mine_x].astype(f32)
            total[owner] = summed.astype(low)

        swap_own(at).start()
        for hop in range(1, n):
            swap_out(at, hop).start()

    swap_rows(0)
    for copy in head_loads:
        copy.wait()

    @pl.loop(0, group)
    def _(head):
        for hop in range(1, n):
            there = do_all.at[head, owned(lax.rem(me + n - hop, n))]
            remote(
                there, there, do_send.at[head, hop], do_recv.at[head, hop], others[hop - 1]
            ).wait_recv()
        for at in range(length // block):
            keys = (at + 1) * block
            here = pl.ds(at * block, block)
            query_all, grad_all = scaled(low_ref[head, here]), do_all[head, here]
            log_all = lse_ref[head, here]
            logs = (log_all[:, 0:1], log_all[:, wide // 2 : wide // 2 + 1])
            dqs, dks, dvs = [], [], []
            for query, grad, log_sum in zip(halves(query_all), halves(grad_all), logs):
                scores = masked(product_back(query, low_ref[group, :keys]))
                probs = jnp.exp(scores - log_sum)
                grad_probs = product_back(grad, low_ref[group + 1, :keys])
                both = probs * grad_probs
                inner = jnp.sum(both, axis=-1, keepdims=True)
                grad_scores = (both - probs * inner).astype(low)
                dqs.append(product(grad_scores, low_ref[group, :keys]))
                dks.append(product_rows(grad_scores, query_all))
                dvs.append(product_rows(probs.astype(low), grad_all))
            dk_sum[:keys] += pack(*dks)
            dv_sum[:keys] += pack(*dvs)
            head_back(pack(*dqs) * score_scale, here, head, 0)
        for hop in range(1, n):
            give(head, hop).start()

        @pl.when(head == 0)
        def _():
            crossing(4).wait_recv()

            @pl.loop(0, n)
            def _(owner):
                summed = o_term[owner, :, mine_core].astype(f32) + o2[owner].astype(f32)
                o_term[owner, :, mine_core] = summed.astype(low)

            crossing(3).start()
            swap_rows(1)

    @pl.loop(0, length // block)
    def _(at):
        here = pl.ds(pl.multiple_of(at * block, block), block)
        head_back(dk_sum[here], here, group, 1)
        d_own[group + 1, here] = dv_sum[here].astype(low)

    for head in (group, group + 1):
        for hop in range(1, n):
            give(head, hop).start()
    keep_d = pltpu.make_async_copy(d_own.at[:, owned(me)], d_out.at[me], own_sem.at[1])
    keep_d.start()
    for copy in loads[8:]:
        copy.wait()

    @pl.loop(0, n // 2)
    def _(pair):
        cols = pl.ds(pl.multiple_of(pair * 2 * shard, 2 * shard), 2 * shard)
        grads = jnp.concatenate([d_own[head] for head in range(group + 2)], axis=1)
        sums = [
            product_rows(h_all[seq, :, :, cols].reshape(length, 2 * shard), grads)
            for seq in (0, 1)
        ]
        both = []
        for head in range(group + 2):
            here = slice(head * wide, (head + 1) * wide)
            packed = pack(sums[0][:, here], sums[1][:, here])
            both.append(packed + pltpu.roll(packed, wide // 2, 1))
        both.append(jnp.zeros_like(both[0]))
        for at in range(0, group + 2, 2):
            part = pack(both[at], both[at + 1]).astype(low).reshape(2, 2, 2, shard // 4, wide)
            q_term[pl.ds(2 * pair, 2), :, :, :, at // 2 * wide : (at // 2 + 1) * wide] = part

    gives = [
        pltpu.make_async_copy(source, target, give_sem.at[at])
        for at, (source, target) in enumerate(
            (
                (d_sum, d_give),
                (q_sum, q_out),
                (o_sum, o_give),
                (g_flat, g_give),
                (u_flat, u_give),
            )
        )
    ]
    crossing(5).start()
    crossing(0).wait_recv()
    piece = d1.shape[1] // 6

    @pl.loop(0, 6)
    def _(at):
        here = pl.ds(pl.multiple_of(at * piece, piece), piece)
        summed = d_sum[here].astype(f32) + d1[mine_x, here].astype(f32)
        d_sum[here] = summed.astype(low)

    gives[0].start()
    crossing(5).wait_recv()

    @pl.loop(0, n)
    def _(owner):
        summed = q_term[owner, :, mine_core].astype(f32) + q2[owner].astype(f32)
        q_sum[owner] = summed.astype(low)

    gives[1].start()
    crossing(3).wait_recv()

    @pl.loop(0, n)
    def _(owner):
        summed = o_sum[owner].astype(f32) + o_term[owner, mine_x, mine_core].astype(f32)
        o_sum[owner] = summed.astype(low)

    gives[2].start()
    for at in range(6):
        crossing(at).wait_send()
    for at in (0, 1):
        swap_own(at).wait()
        for hop in range(1, n):
            swap_out(at, hop).wait()
        swapped, flat = ((g_swap, g_flat), (u_swap, u_flat))[at]
        cols = swapped.shape[2]
        for source in range(n):
            flat[:, source * cols : (source + 1) * cols] = swapped[source]
        gives[3 + at].start()

    @pl.loop(0, group)
    def _(head):
        for hop in range(1, n):
            bring(head, hop).wait_send()

    @pl.loop(0, group + 2)
    def _(head):
        for hop in range(1, n):
            give(head, hop).wait_send()
            there = d_out.at[lax.rem(me + n - hop, n), head]
            remote(
                there, there, d_send.at[head, hop], d_recv.at[head, hop], others[hop - 1]
            ).wait_recv()

    keep_d.wait()
    for copy in gives:
        copy.wait()


def attend_back(low_heads, log_sums, lin, cosine, sine, gain, above, w_output, feed_terms, normed):
    n = lax.axis_size("ctx")
    f32, low = jnp.float32, jnp.bfloat16
    count, length, wide = lin.shape
    group = count - 2
    width = normed.shape[3]
    rows_half, cols_half = feed_terms[0].shape, feed_terms[4].shape
    rows, out_width = above[4].shape
    out_half = (n, 2, rows_half[2], width)
    return pl.pallas_call(
        functools.partial(attend_back_kernel, n, group, 256),
        out_shape=[
            jax.ShapeDtypeStruct((n, count, length // n, wide), low),
            jax.ShapeDtypeStruct((n, 2, rows_half[2], (count + 1) // 2 * wide), low),
            jax.ShapeDtypeStruct(gain.shape, f32),
            jax.ShapeDtypeStruct((rows_half[2], n * rows_half[3]), low),
            jax.ShapeDtypeStruct((rows_half[2], n * rows_half[3]), low),
            jax.ShapeDtypeStruct(cols_half[1:], low),
            jax.ShapeDtypeStruct((n,) + out_half[2:], low),
            jax.ShapeDtypeStruct((rows, width), f32),
            jax.ShapeDtypeStruct((8, width), f32),
        ],
        in_specs=[ANY] * 5 + [VMEM] * 6 + [ANY] * 8,
        out_specs=[ANY, ANY, VMEM] + [ANY] * 4 + [VMEM] * 2,
        scratch_shapes=[
            pltpu.VMEM((n, group, length // n, wide), low),
            pltpu.VMEM((group, length, wide), low),
            pltpu.VMEM((length, wide), f32),
            pltpu.VMEM((length, wide), f32),
        ]
        + [pltpu.VMEM(shape, low) for shape in (rows_half, rows_half, (n,) + rows_half[2:])] * 2
        + [pltpu.VMEM(shape, low) for shape in (cols_half, cols_half)]
        + [pltpu.VMEM((n, 2) + out_half[1:], low), pltpu.VMEM(out_half, low)]
        + [
            pltpu.VMEM((count, length, wide), low),
            pltpu.VMEM((n,) + rows_half[2:], low),
            pltpu.VMEM((n,) + rows_half[2:], low),
            pltpu.VMEM((2, n, length // n, width), low),
            pltpu.VMEM((n, 2, 2, rows_half[2], (count + 1) // 2 * wide), low),
            pltpu.VMEM((n, 2, rows_half[2], (count + 1) // 2 * wide), low),
            pltpu.VMEM((n, 2, rows_half[2], (count + 1) // 2 * wide), low),
            pltpu.VMEM((rows_half[2], n * rows_half[3]), low),
            pltpu.VMEM((rows_half[2], n * rows_half[3]), low),
            pltpu.VMEM(cols_half[1:], low),
            pltpu.VMEM((n,) + out_half[2:], low),
            pltpu.VMEM((rows, width), low),
            pltpu.VMEM(low_heads.shape, low),
            pltpu.VMEM(log_sums.shape, f32),
            pltpu.VMEM(lin.shape, f32),
            pltpu.VMEM(cosine.shape, f32),
            pltpu.VMEM(sine.shape, f32),
        ]
        + [
            pltpu.SemaphoreType.DMA((group, n)),
            pltpu.SemaphoreType.DMA((group, n)),
            pltpu.SemaphoreType.DMA((count, n)),
            pltpu.SemaphoreType.DMA((count, n)),
            pltpu.SemaphoreType.DMA((4,)),
            pltpu.SemaphoreType.DMA((10,)),
            pltpu.SemaphoreType.DMA((6,)),
            pltpu.SemaphoreType.DMA((6,)),
            pltpu.SemaphoreType.DMA((2, n)),
            pltpu.SemaphoreType.DMA((2, n)),
            pltpu.SemaphoreType.DMA((5,)),
            pltpu.SemaphoreType.DMA((5,)),
        ],
        compiler_params=pltpu.CompilerParams(
            collective_id=3, has_side_effects=True, vmem_limit_bytes=VMEM_BYTES
        ),
        cost_estimate=pl.CostEstimate(
            flops=40 * group * length * length * wide, bytes_accessed=2**26, transcendentals=0
        ),
    )(low_heads, log_sums, lin, cosine, sine, gain, *above, w_output, *feed_terms, normed)


def last_kernel(n, widths, x_ref, norm_ref, f_gain, h_gain, q_sum, w_ref, b_ref, o_ref, *refs):
    g_ref, u_ref, d_ref, y_ref = refs[:4]
    dx_out, n_out, y_out, q_all, o_all, g_all, u_all, d_all = refs[4:12]
    q1, q3, q4, q5, n1, n2, n3, n4, o3, o4, blocks, flat, w_all, y_own, y_all = refs[12:27]
    load_sem, x_send, x_recv, a_send, a_recv, own_sem, y_send, y_recv = refs[27:35]
    f_send, f_recv, f_own, o_send, o_recv, o_own, q_send, q_recv, q_own = refs[35:]
    f32, low = jnp.float32, jnp.bfloat16
    me = lax.axis_index("ctx")
    others = [lax.rem(me + hop, n) for hop in range(1, n)]
    mine_x = lax.div(lax.axis_index("rep"), 2)
    core, across = rep_partners()
    loads = (
        pltpu.make_async_copy(q_sum.at[:, mine_x], q1, load_sem.at[0]),
        pltpu.make_async_copy(b_ref, blocks, load_sem.at[1]),
        pltpu.make_async_copy(w_ref, w_all, load_sem.at[2]),
    )
    y_load = pltpu.make_async_copy(y_ref, y_own, load_sem.at[3])
    y_load.start()
    for copy in loads:
        copy.start()
    place = ring_place(me, n)
    toward = (around(place, 1, n), around(place, -1, n))
    y_half = y_own.shape[1] // 2
    y_parts = (pl.ds(0, y_half), pl.ds(y_half, y_half))

    def y_copy(step, side):
        source = y_own if step == 0 else y_all
        return remote(
            source.at[step, y_parts[side]],
            y_all.at[step + 1, y_parts[side]],
            y_send.at[side, step + 1],
            y_recv.at[side, step + 1],
            toward[side],
        )

    def y_hop(step):
        if step > 0:
            for side in (0, 1):
                y_copy(step - 1, side).wait_recv()
            summed = y_all[step].astype(f32) + y_own[step].astype(f32)
            (y_out if step == n - 1 else y_all.at[step])[...] = summed.astype(low)
        if step < n - 1:
            for side in (0, 1):
                y_copy(step, side).start()

    def cross(at, source, target, other):
        return remote(source, target, x_send.at[at], x_recv.at[at], other, "rep")

    steps = (
        cross(0, q_sum.at[:, 1 - mine_x], q3, across),
        cross(1, n1, n2, core),
        cross(2, n2, n3, across),
    )

    def swap_out(at, hop):
        source, target = ((o_ref, o3), (q3, q4), (n3, n4))[at]
        other = others[hop - 1]
        return remote(
            source if at == 2 else source.at[other],
            target.at[me],
            a_send.at[at, hop],
            a_recv.at[at, hop],
            other,
        )

    def swap_own(at):
        source, target = ((o_ref, o3), (q3, q4), (n3, n4))[at]
        return pltpu.make_async_copy(
            source if at == 2 else source.at[me], target.at[me], own_sem.at[at]
        )

    def swap_all(at):
        swap_own(at).start()
        for hop in range(1, n):
            swap_out(at, hop).start()

    def swapped(at):
        swap_own(at).wait()
        for hop in range(1, n):
            swap_out(at, hop).wait()

    few = o4.shape[0]
    quarter = d_ref.shape[1]

    def rows_of(target):
        return lambda r: target.at[pl.ds(pl.multiple_of(r * few, 16), few)]

    feed = RepShare(
        [
            (g_ref, rows_of(g_all)),
            (u_ref, rows_of(u_all)),
            (d_ref, lambda r: d_all.at[:, pl.ds(pl.multiple_of(r * quarter, quarter), quarter)]),
        ],
        f_send,
        f_recv,
        f_own,
    )
    last_q = RepShare([(q5, rows_of(q_all))], q_send, q_recv, q_own)
    last_o = RepShare([(o4, rows_of(o_all))], o_send, o_recv, o_own)

    greet(others, rep_partners())
    steps[0].start()
    feed.begin()
    y_load.wait()
    y_hop(0)
    swap_all(0)
    for copy in loads:
        copy.wait()
    side_by_side(blocks, flat)
    rows, width = x_ref.shape
    tile = 256

    @pl.loop(0, width // tile)
    def _(at):
        cols = pl.ds(pl.multiple_of(at * tile, tile), tile)
        dx_out[:, cols] = product_back(flat[...], w_rows(w_all, at, tile))

    y_hop(1)
    steps[0].wait()

    @pl.loop(0, n)
    def _(owner):
        q3[owner] = (q3[owner].astype(f32) + q1[owner].astype(f32)).astype(low)

    swap_all(1)
    y_hop(2)
    n1[...] = jnp.zeros_like(n1)
    chunk = 64
    totals = jnp.zeros((1, width), f32)
    for at in range(rows // chunk):
        here = pl.ds(at * chunk, chunk)
        x = x_ref[here].astype(f32)
        back, terms = norm_back(dx_out[here], x, norm_ref[...])
        totals += jnp.sum(terms, axis=0, keepdims=True)
        dx_out[here] = back
    lanes = n1.shape[1]
    lines = width // lanes
    for at in range(lines):
        here = slice(at * lanes, (at + 1) * lanes)
        n1[at : at + 1] = totals[:, here]
        n1[lines + at : lines + at + 1] = f_gain[:, here]
    heads = h_gain[0:2]
    heads = heads + pltpu.roll(heads, lanes // 2, 1)
    n1[2 * lines : 2 * lines + 1] = pack(heads[0:1], heads[1:2])
    steps[1].start()
    y_hop(3)
    steps[1].wait()
    n2[...] += n1[...]
    steps[2].start()
    feed.middle(0)
    y_hop(4)
    swapped(1)
    q_wide, k_wide = widths
    for source in range(n):
        at = 0
        place = 0
        for wide in (q_wide, k_wide, k_wide):
            start = place + source * wide
            q5[:, start : start + wide] = q4[source, :, at : at + wide]
            at += wide
            place += n * wide
    last_q.begin()
    y_hop(5)
    feed.middle(1)
    swapped(0)

    @pl.loop(0, few // 16)
    def _(at):
        here = pl.ds(pl.multiple_of(at * 16, 16), 16)
        total = o3[0, here].astype(f32)
        for source in range(1, n):
            total += o3[source, here].astype(f32)
        o4[here] = total.astype(low)

    last_o.begin()
    y_hop(6)
    steps[2].wait()
    n3[...] += n2[...]
    swap_all(2)
    feed.middle(2)
    last_q.middle()
    last_o.middle()
    for step in range(7, n):
        y_hop(step)
    swapped(2)
    total = n4[0]
    for source in range(1, n):
        total += n4[source]
    n_out[...] = total
    feed.end()
    last_q.end()
    last_o.end()
    for step in range(n - 1):
        for side in (0, 1):
            y_copy(step, side).wait_send()


def w_rows(w_all, at, tile):
    n, reps, few, cols = w_all.shape
    rows = [w_all[lax.div(at * tile + start, reps * few), lax.rem(lax.div(at * tile + start, few), reps),
                  pl.ds(pl.multiple_of(lax.rem(at * tile + start, few), 16), 16)]
            for start in range(0, tile, 16)]
    return jnp.concatenate(rows, axis=0)


def last_sums(x, norm_gain, ffn_terms, head_terms, q_sum, w_full, blocks, parts, widths):
    o_part, g_part, u_part, d_part, y_part = parts
    n = lax.axis_size("ctx")
    reps = lax.axis_size("rep")
    f32, low = jnp.float32, jnp.bfloat16
    few, wide = q_sum.shape[2:]
    rows, width = x.shape
    shard = reps * few
    out_wide = o_part.shape[2]
    feed_wide = g_part.shape[1]
    lines = -(-(2 * width // 128 + 1) // 8) * 8
    return pl.pallas_call(
        functools.partial(last_kernel, n, widths),
        out_shape=[
            jax.ShapeDtypeStruct((rows, width), f32),
            jax.ShapeDtypeStruct((lines, 128), f32),
            jax.ShapeDtypeStruct(y_part.shape[1:], low),
            jax.ShapeDtypeStruct((shard, w_full.shape[3]), low),
            jax.ShapeDtypeStruct((shard, out_wide), low),
            jax.ShapeDtypeStruct((shard, feed_wide), low),
            jax.ShapeDtypeStruct((shard, feed_wide), low),
            jax.ShapeDtypeStruct((d_part.shape[0], reps * d_part.shape[1]), low),
        ],
        in_specs=[VMEM] * 4 + [ANY] * 8,
        out_specs=[VMEM] * 3 + [ANY] * 5,
        scratch_shapes=[
            pltpu.VMEM((n, few, wide), low),
            pltpu.VMEM((n, few, wide), low),
            pltpu.VMEM((n, few, wide), low),
            pltpu.VMEM((few, w_full.shape[3]), low),
            pltpu.VMEM((lines, 128), f32),
            pltpu.VMEM((lines, 128), f32),
            pltpu.VMEM((lines, 128), f32),
            pltpu.VMEM((n, lines, 128), f32),
            pltpu.VMEM((n, few, out_wide), low),
            pltpu.VMEM((few, out_wide), low),
            pltpu.VMEM(blocks.shape, low),
            pltpu.VMEM((rows, w_full.shape[3]), low),
            pltpu.VMEM(w_full.shape, low),
            pltpu.VMEM(y_part.shape, low),
            pltpu.VMEM(y_part.shape, low),
            pltpu.SemaphoreType.DMA((4,)),
            pltpu.SemaphoreType.DMA((3,)),
            pltpu.SemaphoreType.DMA((3,)),
            pltpu.SemaphoreType.DMA((3, n)),
            pltpu.SemaphoreType.DMA((3, n)),
            pltpu.SemaphoreType.DMA((3,)),
            pltpu.SemaphoreType.DMA((2, n)),
            pltpu.SemaphoreType.DMA((2, n)),
        ]
        + [
            pltpu.SemaphoreType.DMA(shape)
            for k in (3, 1, 1)
            for shape in ((k, 3), (k, 3), (k,))
        ],
        compiler_params=pltpu.CompilerParams(
            collective_id=4, has_side_effects=True, vmem_limit_bytes=VMEM_BYTES
        ),
    )(x, norm_gain, ffn_terms, head_terms, q_sum, w_full, blocks, *parts)


def feed_kernel(n, tile, normed_ref, grad_ref, wg_src, wu_src, wd_src, wq_ref, *refs):
    y_out, y_hold, b_out, wq_out, g_keep, g_got, u_keep, u_got, d_keep, d_got = refs[:10]
    h_slots, d_slots, y_slots, b_slots, hid, dgate, dup, dwg, dwu, dwd, stage, d_stage, y_stage = refs[10:23]
    wg_ref, wu_ref, wd_ref = refs[23:26]
    h_send, h_recv, y_send, y_recv, b_send, b_recv, d_sem, own_sem, r_send, r_recv, r_own = refs[26:37]
    keep_sem, c_send, c_recv, dc_send, dc_recv, y_sem = refs[37:]
    f32, low = jnp.float32, jnp.bfloat16
    me = lax.axis_index("ctx")
    place = ring_place(me, n)
    right, left = around(place, 1, n), around(place, -1, n)
    rows, width = normed_ref.shape
    half = rows // 2
    parts = (pl.ds(0, half), pl.ds(half, half))
    toward = (right, left)

    def grad_load(step, side):
        owner = around(place, -1 - step if side == 0 else 1 + step, n)
        return pltpu.make_async_copy(
            grad_ref.at[owner, parts[side]],
            d_slots.at[lax.rem(step, 2), parts[side]],
            d_sem.at[lax.rem(step, 2), side],
        )

    def pass_on(step, side):
        return remote(
            h_slots.at[step, parts[side]],
            h_slots.at[step + 1, parts[side]],
            h_send.at[side, step + 1],
            h_recv.at[side, step + 1],
            toward[side],
        )

    def sum_on(slots, send, recv, step, side):
        return remote(
            slots.at[step, parts[side]],
            slots.at[step + 1, parts[side]],
            send.at[side, step + 1],
            recv.at[side, step + 1],
            toward[side],
        )

    def first(side):
        return remote(
            normed_ref.at[parts[side]],
            h_slots.at[0, parts[side]],
            h_send.at[side, 0],
            h_recv.at[side, 0],
            toward[side],
        )

    weight_loads = [
        pltpu.make_async_copy(source, target, own_sem.at[5 + at])
        for at, (source, target) in enumerate(
            ((wg_src, wg_ref), (wu_src, wu_ref), (wd_src, wd_ref))
        )
    ]
    for copy in weight_loads:
        copy.start()
    for side in (0, 1):
        grad_load(0, side).start()
    keep = pltpu.make_async_copy(normed_ref, h_slots.at[n - 1], own_sem.at[0])
    keep.start()
    share = RepShare([(wq_ref, lambda r: wq_out.at[:, r])], r_send, r_recv, r_own)
    greet((left, right), rep_partners())
    for side in (0, 1):
        first(side).start()
    share.begin()
    y_slots[0] = jnp.zeros(y_slots.shape[1:], low)
    b_slots[0] = jnp.zeros((rows, width), low)

    @pl.loop(0, width // tile)
    def _(at):
        cols = pl.ds(pl.multiple_of(at * tile, tile), tile)
        dwg[cols, :] = jnp.zeros((tile, dwg.shape[1]), f32)
        dwu[cols, :] = jnp.zeros((tile, dwu.shape[1]), f32)
        dwd[:, cols] = jnp.zeros((dwd.shape[0], tile), f32)

    keep.wait()
    for copy in weight_loads:
        copy.wait()

    def next_block(step):
        for side in (0, 1):
            block = h_slots.at[step, parts[side]]
            remote(block, block, h_send.at[side, step], h_recv.at[side, step], right).wait_recv()

            @pl.when(step < n - 2)
            def _():
                pass_on(step, side).start()

    def hold(step):
        turn = lax.rem(step, 2)
        return pltpu.make_async_copy(y_stage.at[turn], y_hold.at[step], y_sem.at[turn])

    next_block(0)
    kept = y_slots.shape[2] // tile

    @pl.loop(0, n)
    def _(step):
        @pl.when(step < n - 1)
        def _():
            for side in (0, 1):
                grad_load(step + 1, side).start()

        for side in (0, 1):
            grad_load(step, side).wait()

        @pl.when(step == n // 2)
        def _():
            share.middle()

        turn = lax.rem(step, 2)
        h = h_slots[step]
        gate = jnp.dot(h, wg_ref[...], preferred_element_type=f32)
        up = jnp.dot(h, wu_ref[...], preferred_element_type=f32)
        grad_hidden = product_back(d_slots[turn], wd_ref[...])
        sigma = jax.nn.sigmoid(gate)
        silu = gate * sigma
        hid[...] = (silu * up).astype(low)
        dup[...] = (grad_hidden * silu).astype(low)
        dgate[...] = (grad_hidden * up * sigma * (1.0 + gate * (1.0 - sigma))).astype(low)

        @pl.when(step < n - 2)
        def _():
            next_block(step + 1)

        @pl.when(step > 0)
        def _():
            for side in (0, 1):
                sum_on(b_slots, b_send, b_recv, step - 1, side).wait_recv()

        @pl.loop(0, width // tile)
        def _(at):
            cols = pl.ds(pl.multiple_of(at * tile, tile), tile)
            back = product_back(dgate[...], wg_ref[cols, :]) + product_back(
                dup[...], wu_ref[cols, :]
            )
            b_slots[step, :, cols] = (b_slots[step, :, cols].astype(f32) + back).astype(low)

        @pl.when(step < n - 1)
        def _():
            for side in (0, 1):
                sum_on(b_slots, b_send, b_recv, step, side).start()

        @pl.when(step > 0)
        def _():
            for side in (0, 1):
                sum_on(y_slots, y_send, y_recv, step - 1, side).wait_recv()

        @pl.loop(0, kept)
        def _(at):
            cols = pl.ds(pl.multiple_of(at * tile, tile), tile)
            added = jnp.dot(hid[...], wd_ref[:, cols], preferred_element_type=f32)
            y_slots[step, :, cols] = (y_slots[step, :, cols].astype(f32) + added).astype(low)

        @pl.when(step < n - 1)
        def _():
            for side in (0, 1):
                sum_on(y_slots, y_send, y_recv, step, side).start()

        @pl.when(step >= 2)
        def _():
            hold(step - 2).wait()

        @pl.loop(kept, width // tile)
        def _(at):
            cols = pl.ds(pl.multiple_of(at * tile, tile), tile)
            there = pl.ds(pl.multiple_of((at - kept) * tile, tile), tile)
            added = jnp.dot(hid[...], wd_ref[:, cols], preferred_element_type=f32)
            y_stage[turn, :, there] = added.astype(low)

        hold(step).start()

        @pl.loop(0, width // tile)
        def _(at):
            cols = pl.ds(pl.multiple_of(at * tile, tile), tile)
            h_cols = h_slots[step, :, cols]
            dwg[cols, :] += product_rows(h_cols, dgate[...])
            dwu[cols, :] += product_rows(h_cols, dup[...])
            dwd[:, cols] += product_rows(hid[...], d_slots[turn, :, cols])

    outs = (
        pltpu.make_async_copy(y_slots.at[n - 1], y_out, own_sem.at[1]),
        pltpu.make_async_copy(b_slots.at[n - 1], b_out, own_sem.at[2]),
    )
    for copy in outs:
        copy.start()
    hold(n - 2).wait()
    hold(n - 1).wait()
    core, _ = rep_partners()
    mine = lax.rem(lax.axis_index("rep"), 2)
    wide = width // 4
    few = g_keep.shape[2]

    def column_copies(side):
        quarter = (2 * side + mine, 2 * side + 1 - mine)
        return quarter, (
            pltpu.make_async_copy(d_stage.at[2 * side], d_keep.at[side], own_sem.at[3 + side]),
            remote(
                d_stage.at[2 * side + 1],
                d_got.at[side],
                dc_send.at[side],
                dc_recv.at[side],
                core,
                "rep",
            ),
        )

    for side in (0, 1):
        quarters, copies = column_copies(side)
        for at, (quarter, copy) in enumerate(zip(quarters, copies)):
            cols = pl.ds(pl.multiple_of(quarter * wide, wide), wide)
            d_stage[2 * side + at] = dwd[:, cols].astype(low)
            copy.start()

    def row_copies(owner, turn):
        for at, (total, keep, got) in enumerate(((dwg, g_keep, g_got), (dwu, u_keep, u_got))):
            for side in (0, 1):
                slot = 4 * at + 2 * side
                yield total, slot, 2 * side + mine, pltpu.make_async_copy(
                    stage.at[turn, slot], keep.at[owner, side], keep_sem.at[turn, slot // 2]
                )
                yield total, slot + 1, 2 * side + 1 - mine, remote(
                    stage.at[turn, slot + 1],
                    got.at[owner, side],
                    c_send.at[owner, slot // 2],
                    c_recv.at[owner, slot // 2],
                    core,
                    "rep",
                )

    def row_wait(owner, turn):
        for _, slot, _, copy in row_copies(owner, turn):
            if slot % 2 == 0:
                copy.wait()
            else:
                copy.wait_send()

    @pl.loop(0, n)
    def _(owner):
        turn = lax.rem(owner, 2)

        @pl.when(owner >= 2)
        def _():
            row_wait(owner - 2, turn)

        for total, slot, quarter, copy in row_copies(owner, turn):
            start = pl.multiple_of((4 * owner + quarter) * few, 8)
            stage[turn, slot] = total[pl.ds(start, few), :].astype(low)
            copy.start()

    for owner in (n - 2, n - 1):
        row_wait(owner, owner % 2)

    @pl.loop(0, n)
    def _(owner):
        for _, slot, _, copy in row_copies(owner, 0):
            if slot % 2 == 1:
                copy.wait_recv()

    for side in (0, 1):
        for copy in column_copies(side)[1]:
            copy.wait()
    for copy in outs:
        copy.wait()
    share.end()
    for side in (0, 1):
        first(side).wait_send()

        @pl.loop(0, n - 2)
        def _(step):
            pass_on(step, side).wait_send()

        @pl.loop(0, n - 1)
        def _(step):
            sum_on(b_slots, b_send, b_recv, step, side).wait_send()
            sum_on(y_slots, y_send, y_recv, step, side).wait_send()


def feed_scratch(n, rows, width, cols):
    low = jnp.bfloat16
    return [
        pltpu.VMEM((n, rows, width), low),
        pltpu.VMEM((2, rows, width), low),
        pltpu.VMEM((n, rows, width // 2), low),
        pltpu.VMEM((n, rows, width), low),
        pltpu.VMEM((rows, cols), low),
        pltpu.VMEM((rows, cols), low),
        pltpu.VMEM((rows, cols), low),
        pltpu.VMEM((width, cols), jnp.float32),
        pltpu.VMEM((width, cols), jnp.float32),
        pltpu.VMEM((cols, width), jnp.float32),
        pltpu.VMEM((2, 8, width // (4 * n), cols), low),
        pltpu.VMEM((4, cols, width // 4), low),
        pltpu.VMEM((2, rows, width // 2), low),
        pltpu.VMEM((width, cols), low),
        pltpu.VMEM((width, cols), low),
        pltpu.VMEM((cols, width), low),
    ]


def feed_fits(n, rows, width, cols):
    wide = -(-cols // 128) * 128
    slots = (3 * n + 2) * rows * width * 2 + 3 * rows * wide * 2
    weights = 3 * width * wide * (2 + 4) + 4 * width * wide * 2 // n + width * wide * 2
    return slots + weights + 24 * rows * wide <= VMEM_BYTES


def feed_ring(normed, grad_all, w_gate, w_up, w_down, quarter):
    n = lax.axis_size("ctx")
    rows, width = normed.shape
    cols = w_gate.shape[1]
    low = jnp.bfloat16
    reps = lax.axis_size("rep")
    return pl.pallas_call(
        functools.partial(feed_kernel, n, 256),
        out_shape=[
            jax.ShapeDtypeStruct((rows, width // 2), low),
            jax.ShapeDtypeStruct((n, rows, width // 2), low),
            jax.ShapeDtypeStruct((rows, width), low),
            jax.ShapeDtypeStruct((n, reps) + quarter.shape[1:], quarter.dtype),
        ]
        + [jax.ShapeDtypeStruct((n, 2, width // (4 * n), cols), low)] * 4
        + [jax.ShapeDtypeStruct((2, cols, width // 4), low)] * 2,
        in_specs=[ANY] * 6,
        out_specs=[ANY] * 10,
        scratch_shapes=feed_scratch(n, rows, width, cols)
        + [pltpu.SemaphoreType.DMA((2, n))] * 6
        + [pltpu.SemaphoreType.DMA((2, 2)), pltpu.SemaphoreType.DMA((8,))]
        + [pltpu.SemaphoreType.DMA((1, 3))] * 2
        + [pltpu.SemaphoreType.DMA((1,))]
        + [pltpu.SemaphoreType.DMA((2, 4))]
        + [pltpu.SemaphoreType.DMA((n, 4))] * 2
        + [pltpu.SemaphoreType.DMA((2,))] * 3,
        compiler_params=pltpu.CompilerParams(
            collective_id=1, has_side_effects=True, vmem_limit_bytes=VMEM_BYTES
        ),
        cost_estimate=pl.CostEstimate(
            flops=18 * n * rows * width * cols, bytes_accessed=40 * width * cols, transcendentals=0
        ),
    )(normed, grad_all, w_gate, w_up, w_down, quarter)


def columns_by_owner(shard, parts):
    rows, width = shard.shape
    return shard.reshape(rows, parts, width // parts).transpose(1, 0, 2)


def columns_joined(blocks):
    parts, rows, width = blocks.shape
    return blocks.transpose(1, 0, 2).reshape(rows, parts * width)


def take_gains(gains, width):
    gains = gains.astype(jnp.float32)
    return gains[:width, 0], gains[:width, 1], gains[width:, 0], gains[width:, 1]


class HeadAttention:
    def __init__(self, dims, shards, feed_shards, w_down, gains_shard, tokens, cotangent):
        self.dims = dims
        parts, seqs, span, width, head_dim, heads, kv_heads = dims
        low = jnp.bfloat16
        group = heads // kv_heads
        self.group = group
        rows = seqs * span
        length = parts * span
        few = gains_shard.shape[0]
        padded = jnp.pad(gains_shard.astype(low).astype(jnp.float32).T, ((0, 6), (0, -few % 128)))
        (
            self.normed,
            self.lin,
            gains_all,
            out_quarter,
            self.quarter,
            w_gate,
            w_up,
            self.w_down,
        ) = enter(tokens.reshape(rows, width), padded, shards, feed_shards, w_down, head_dim)
        gains = gains_all[:, :2, :few].transpose(0, 2, 1).reshape(-1, 2)
        self.gain_attn, self.gain_ffn, gain_query, gain_key = take_gains(gains, width)
        self.cosine, self.sine = (
            jnp.asarray(table) for table in rotary_constants(length, head_dim, seqs)
        )
        self.gain = jnp.pad(
            jnp.stack([jnp.concatenate([g] * seqs) for g in (gain_query, gain_key)]), ((0, 6), (0, 0))
        )
        self.tokens = tokens.reshape(rows, width)
        (
            self.low_heads,
            self.log_sums,
            self.attended,
            self.resid,
            self.normed_two,
            self.grad_all,
            w_output,
        ) = attend(
            self.lin,
            self.cosine,
            self.sine,
            self.gain,
            self.tokens,
            self.gain_ffn[None],
            cotangent.reshape(rows, width),
            out_quarter,
        )
        self.w_output = w_output.reshape(width, -1)
        self.w_gate = w_gate.reshape(width, -1)
        self.w_up = w_up.reshape(width, -1)

    def feed(self):
        self.added, self.held, back, self.w_full, *self.feed_terms = feed_ring(
            self.normed_two, self.grad_all, self.w_gate, self.w_up, self.w_down, self.quarter
        )
        return back

    def backward(self, normed_two_grad, grad_low):
        span, width = self.dims[2:4]
        self.blocks, self.q_sum, self.head_terms, *parts_done, grad_resid, ffn_terms = attend_back(
            self.low_heads,
            self.log_sums,
            self.lin,
            self.cosine,
            self.sine,
            self.gain,
            (normed_two_grad, self.resid, grad_low, self.gain_ffn[None], self.attended),
            self.w_output.reshape(-1, span, width),
            self.feed_terms,
            self.normed,
        )
        self.parts_done = parts_done
        return grad_resid, ffn_terms[0]

    def finish(self, grad_resid, ffn_terms):
        parts, seqs, span, width, head_dim, heads, kv_heads = self.dims
        gate, up, down, out = self.parts_done
        back, gains, added, mixed, out, gate, up, down = last_sums(
            self.tokens,
            self.gain_attn[None],
            ffn_terms[None],
            self.head_terms,
            self.q_sum,
            self.w_full,
            self.blocks,
            (out, gate, up, down, self.held),
            (self.group * head_dim, head_dim),
        )
        gains = gains.reshape(-1)
        one, two = gains[:width], gains[width : 2 * width]
        query = gains[2 * width : 2 * width + head_dim]
        key = gains[2 * width + head_dim : 2 * width + 2 * head_dim]
        gains = jnp.stack([jnp.concatenate([one, query]), jnp.concatenate([two, key])], axis=1)
        count = gains.shape[0] // parts
        gains = lax.dynamic_slice_in_dim(gains, lax.axis_index("ctx") * count, count, 0)
        cuts = (heads * head_dim, (heads + kv_heads) * head_dim)
        grads = (
            mixed[:, : cuts[0]], mixed[:, cuts[0] : cuts[1]], mixed[:, cuts[1] :], out, gate, up, down, gains
        )
        added = jnp.concatenate([self.added, added], axis=1).astype(jnp.float32)
        return grad_resid + back, self.resid + added, grads


class RowAttention:
    def __init__(self, dims, shards, feed_shards, w_down, gains_shard, tokens, cotangent):
        self.dims = dims
        parts, seqs, span, width, head_dim, heads, kv_heads = dims
        low = jnp.bfloat16
        gains = lax.all_gather(gains_shard.astype(low), "ctx", axis=0, tiled=True)
        self.gain_attn, self.gain_ffn, self.gain_query, self.gain_key = take_gains(gains, width)
        place = lax.axis_index("ctx")
        rows = seqs * span
        self.group = heads // kv_heads
        self.weights = tuple(
            lax.all_gather(w.astype(low), "ctx", axis=0, tiled=True) for w in shards[:3]
        )
        self.w_output = lax.all_gather(shards[3].astype(low), "ctx", axis=0, tiled=True)
        self.w_gate, self.w_up = (
            swap(columns_by_owner(w.astype(low), parts)).reshape(width, -1) for w in feed_shards
        )
        self.w_down = w_down.astype(low)
        self.grad_all = gather(cotangent.reshape(rows, width))
        inputs = tokens.astype(jnp.float32).reshape(rows, width)
        self.normed = (inputs * rms_scale(inputs) * self.gain_attn).astype(jnp.bfloat16)
        query_lin, key_lin, value_lin = (product(self.normed, w) for w in self.weights)
        self.cosine, self.sine = rotary_tables(place * span, span, head_dim)
        self.query_heads = query_lin.reshape(seqs, span, heads, head_dim)
        query_low = rotate(
            self.query_heads * rms_scale(self.query_heads) * self.gain_query, self.cosine, self.sine
        ).astype(jnp.bfloat16)
        self.key_heads = key_lin.reshape(seqs, span, kv_heads, head_dim)
        key_low = rotate(
            self.key_heads * rms_scale(self.key_heads) * self.gain_key, self.cosine, self.sine
        ).astype(jnp.bfloat16)
        kv_width = kv_heads * head_dim
        self.keys_all = lax.all_gather(
            key_low.reshape(seqs, span, kv_width), "ctx", axis=1, tiled=True
        )
        self.values_all = lax.all_gather(
            value_lin.astype(jnp.bfloat16).reshape(seqs, span, kv_width), "ctx", axis=1, tiled=True
        )
        self.query_grouped = query_low.reshape(seqs, span, kv_heads, self.group, head_dim)
        query_pos = place * span + jnp.arange(span)
        self.visible = jnp.arange(parts * span)[None, :] <= query_pos[:, None]
        self.attended = self.forward()
        self.resid = inputs + product(self.attended, self.w_output)
        normed_two = self.resid * rms_scale(self.resid) * self.gain_ffn
        self.normed_two = normed_two.astype(jnp.bfloat16)
        self.tokens = inputs

    def feed(self):
        self.added, back, *self.feed_terms = feed_plain(
            self.normed_two, self.grad_all, self.w_gate, self.w_up, self.w_down
        )
        return back

    def head_scores(self, index):
        head_dim = self.dims[4]
        query_group = lax.dynamic_index_in_dim(self.query_grouped, index, 2, keepdims=False)
        key_group = lax.dynamic_slice_in_dim(self.keys_all, index * head_dim, head_dim, 2)
        value_group = lax.dynamic_slice_in_dim(self.values_all, index * head_dim, head_dim, 2)
        raw = (
            jnp.einsum("scjd,skd->sjck", query_group, key_group, preferred_element_type=jnp.float32)
            * score_scale
        )
        return (query_group, key_group, value_group, jnp.where(self.visible, raw, -1e30))

    def forward(self):
        parts, seqs, span, width, head_dim, heads, kv_heads = self.dims

        def forward_head(index, carry):
            attended, log_sums = carry
            _, _, value_group, scores = self.head_scores(index)
            top = jnp.max(scores, axis=-1, keepdims=True)
            expo = jnp.exp(scores - top)
            total = jnp.sum(expo, axis=-1, keepdims=True)
            probs = (expo / total).astype(jnp.bfloat16)
            head_out = jnp.einsum(
                "sjck,skd->scjd", probs, value_group, preferred_element_type=jnp.float32
            )
            attended = lax.dynamic_update_index_in_dim(attended, head_out, index, 2)
            log_sums = lax.dynamic_update_index_in_dim(
                log_sums, (top + jnp.log(total))[..., 0], index, 0
            )
            return (attended, log_sums)

        attended, self.log_sums = lax.fori_loop(
            0,
            kv_heads,
            forward_head,
            (
                jnp.zeros((seqs, span, kv_heads, self.group, head_dim), jnp.float32),
                jnp.zeros((kv_heads, seqs, self.group, span), jnp.float32),
            ),
        )
        return attended.reshape(seqs * span, heads * head_dim).astype(jnp.bfloat16)

    def backward(self, normed_two_grad, grad_low):
        back_two, ffn_terms = norm_back(
            normed_two_grad.astype(jnp.float32), self.resid, self.gain_ffn
        )
        grad_resid = grad_low.astype(jnp.float32) + back_two
        resid_low = grad_resid.astype(jnp.bfloat16)
        self.out_term = product_rows(self.attended, resid_low)
        self.heads_backward(product_back(resid_low, self.w_output).astype(jnp.bfloat16))
        return grad_resid, jnp.sum(ffn_terms, axis=0)

    def heads_backward(self, grad_rows):
        parts, seqs, span, width, head_dim, heads, kv_heads = self.dims
        group = self.group
        rows = seqs * span
        length = parts * span
        kv_width = kv_heads * head_dim
        grad_grouped = grad_rows.reshape(seqs, span, kv_heads, group, head_dim)

        def backward_head(index, carry):
            query_acc, key_acc, value_acc = carry
            query_group, key_group, value_group, scores = self.head_scores(index)
            log_group = lax.dynamic_index_in_dim(self.log_sums, index, 0, keepdims=False)
            probs = jnp.exp(scores - log_group[..., None])
            grad_group = lax.dynamic_index_in_dim(grad_grouped, index, 2, keepdims=False)
            grad_probs = jnp.einsum(
                "scjd,skd->sjck", grad_group, value_group, preferred_element_type=jnp.float32
            )
            inner = jnp.sum(probs * grad_probs, axis=-1, keepdims=True)
            grad_scores = (probs * (grad_probs - inner)).astype(jnp.bfloat16)
            grad_query = (
                jnp.einsum(
                    "sjck,skd->scjd", grad_scores, key_group, preferred_element_type=jnp.float32
                )
                * score_scale
            )
            grad_key = (
                jnp.einsum(
                    "sjck,scjd->skd", grad_scores, query_group, preferred_element_type=jnp.float32
                )
                * score_scale
            )
            grad_value = jnp.einsum(
                "sjck,scjd->skd",
                probs.astype(jnp.bfloat16),
                grad_group,
                preferred_element_type=jnp.float32,
            )
            query_acc = lax.dynamic_update_index_in_dim(query_acc, grad_query, index, 2)
            key_acc = lax.dynamic_update_slice_in_dim(key_acc, grad_key, index * head_dim, 2)
            value_acc = lax.dynamic_update_slice_in_dim(value_acc, grad_value, index * head_dim, 2)
            return (query_acc, key_acc, value_acc)

        query_acc, key_acc, value_acc = lax.fori_loop(
            0,
            kv_heads,
            backward_head,
            (
                jnp.zeros((seqs, span, kv_heads, group, head_dim), jnp.float32),
                jnp.zeros((seqs, length, kv_width), jnp.float32),
                jnp.zeros((seqs, length, kv_width), jnp.float32),
            ),
        )
        key_back, value_back = (
            lax.psum_scatter(
                acc.astype(jnp.bfloat16), "ctx", scatter_dimension=1, tiled=True
            ).astype(jnp.float32)
            for acc in (key_acc, value_acc)
        )
        query_rot = rotate_back(
            query_acc.reshape(seqs, span, heads, head_dim), self.cosine, self.sine
        )
        query_back, query_gain_terms = norm_back(query_rot, self.query_heads, self.gain_query)
        key_rot = rotate_back(
            key_back.reshape(seqs, span, kv_heads, head_dim), self.cosine, self.sine
        )
        key_grad, key_gain_terms = norm_back(key_rot, self.key_heads, self.gain_key)
        lows = (
            query_back.reshape(rows, heads * head_dim).astype(jnp.bfloat16),
            key_grad.reshape(rows, kv_width).astype(jnp.bfloat16),
            value_back.reshape(rows, kv_width).astype(jnp.bfloat16),
        )
        normed_grad = sum(product_back(g, w) for g, w in zip(lows, self.weights))
        self.grads = tuple(
            rep_sum(
                lax.psum_scatter(
                    product_rows(self.normed, g).astype(jnp.bfloat16),
                    "ctx",
                    scatter_dimension=0,
                    tiled=True,
                )
            )
            for g in lows
        )
        gain_terms = (
            jnp.sum(query_gain_terms, axis=(0, 1, 2)),
            jnp.sum(key_gain_terms, axis=(0, 1, 2)),
        )
        self.normed_grad, self.gain_terms = normed_grad, gain_terms

    def finish(self, grad_resid, ffn_terms):
        back_one, attn_terms = norm_back(self.normed_grad, self.tokens, self.gain_attn)
        query_gain, key_gain = self.gain_terms
        column_one = jnp.concatenate([jnp.sum(attn_terms, axis=0), query_gain])
        column_two = jnp.concatenate([ffn_terms, key_gain])
        grads = self.weight_grads(jnp.stack([column_one, column_two], axis=1))
        return grad_resid + back_one, self.resid + self.added.astype(jnp.float32), grads

    def weight_grads(self, gains_term):
        parts = self.dims[0]
        reps = lax.axis_size("rep")
        shard = self.dims[3] // parts
        out = swap(rep_scatter(owner_blocks(self.out_term, parts, reps)))
        out = jnp.sum(out.astype(jnp.float32), axis=0).astype(jnp.bfloat16)
        gate, up, down = self.feed_terms
        gate, up = (
            rep_gather(columns_joined(swap(rep_scatter(owner_blocks(term, parts, reps)))))
            for term in (gate, up)
        )
        down = rep_gather(rep_scatter(down.reshape(reps, -1, down.shape[1])))
        gains = rep_sum(lax.psum_scatter(gains_term, "ctx", scatter_dimension=0, tiled=True))
        return self.grads + (
            rep_gather(out).reshape(shard, -1),
            gate.reshape(shard, -1),
            up.reshape(shard, -1),
            down.reshape(-1, down.shape[2]),
            gains,
        )


def feed_plain(normed, grad_all, w_gate, w_up, w_down):
    low = jnp.bfloat16
    rows, width = normed.shape
    parts = lax.axis_size("ctx")
    normed_all = gather(normed).reshape(parts * rows, width)
    grad_all = grad_all.reshape(parts * rows, width)
    gate = product(normed_all, w_gate)
    up = product(normed_all, w_up)
    sigma = jax.nn.sigmoid(gate)
    hidden_low = (gate * sigma * up).astype(low)
    added = scatter_sum(product(hidden_low, w_down).astype(low).reshape(parts, rows, width))
    grad_hidden = product_back(grad_all, w_down)
    up_grad_low = (grad_hidden * gate * sigma).astype(low)
    gate_grad_low = (grad_hidden * up * sigma * (1.0 + gate * (1.0 - sigma))).astype(low)
    back = product_back(gate_grad_low, w_gate) + product_back(up_grad_low, w_up)
    return (
        added,
        scatter_sum(back.astype(low).reshape(parts, rows, width)),
        product_rows(normed_all, gate_grad_low),
        product_rows(normed_all, up_grad_low),
        product_rows(hidden_low, grad_all),
    )


def owner_blocks(term, parts, reps):
    rows, cols = term.shape
    return term.reshape(parts, reps, rows // (parts * reps), cols).transpose(1, 0, 2, 3)


def body(

    tokens,
    cotangent,
    query_weight,
    key_weight,
    value_weight,
    output_weight,
    gate_weight,
    up_weight,
    down_weight,
    norm_gains,
    first_query,
    first_key,
    first_value,
    first_output,
    first_gate,
    first_up,
    first_down,
    first_gains,
    second_query,
    second_key,
    second_value,
    second_output,
    second_gate,
    second_up,
    second_down,
    second_gains,
):
    seqs, span, width = tokens.shape
    rows = seqs * span
    head_dim = HD
    heads = query_weight.shape[1] // head_dim
    kv_heads = key_weight.shape[1] // head_dim
    parts = lax.axis_size("ctx")
    dims = (parts, seqs, span, width, head_dim, heads, kv_heads)
    low = jnp.bfloat16
    reps = lax.axis_size("rep")
    packs = parts == kv_heads and reps == 4 and seqs * head_dim == 128
    packs = packs and feed_fits(parts, rows, width, down_weight.shape[0])
    attention = (HeadAttention if packs else RowAttention)(
        dims,
        (query_weight, key_weight, value_weight, output_weight),
        (gate_weight, up_weight),
        down_weight,
        norm_gains,
        tokens,
        cotangent,
    )
    grad_low = cotangent.reshape(rows, width)
    grad_resid, ffn_terms = attention.backward(attention.feed(), grad_low)
    weights = (
        query_weight,
        key_weight,
        value_weight,
        output_weight,
        gate_weight,
        up_weight,
        down_weight,
        norm_gains,
    )
    firsts = (
        first_query,
        first_key,
        first_value,
        first_output,
        first_gate,
        first_up,
        first_down,
        first_gains,
    )
    seconds = (
        second_query,
        second_key,
        second_value,
        second_output,
        second_gate,
        second_up,
        second_down,
        second_gains,
    )
    rates = (0.05, 0.05, 0.05, 0.3, 0.05, 0.05, 0.05, 0.5)
    decays = (0.1, 0.1, 0.1, 0.1, 0.1, 0.1, 0.1, 0.0)
    input_gradient, activations, grads = attention.finish(grad_resid, ffn_terms)
    activations = activations.astype(low).reshape(seqs, span, width)
    input_gradient = input_gradient.reshape(seqs, span, width)
    updated = [
        adamw(w, g.astype(jnp.float32), m, u, rate, decay)
        for w, g, m, u, rate, decay in zip(weights, grads, firsts, seconds, rates, decays)
    ]
    return (
        activations,
        input_gradient,
        updated[0][0],
        updated[1][0],
        updated[2][0],
        updated[3][0],
        updated[4][0],
        updated[5][0],
        updated[6][0],
        updated[7][0],
        updated[0][1],
        updated[1][1],
        updated[2][1],
        updated[3][1],
        updated[4][1],
        updated[5][1],
        updated[6][1],
        updated[7][1],
        updated[0][2],
        updated[1][2],
        updated[2][2],
        updated[3][2],
        updated[4][2],
        updated[5][2],
        updated[6][2],
        updated[7][2],
    )


def solution(mesh):
    placed = (
        P("rep", "ctx", None),
        P("rep", "ctx", None),
        P("ctx", None),
        P("ctx", None),
        P("ctx", None),
        P("ctx", None),
        P("ctx", None),
        P("ctx", None),
        P("ctx", None),
        P("ctx", None),
        P("ctx", None),
        P("ctx", None),
        P("ctx", None),
        P("ctx", None),
        P("ctx", None),
        P("ctx", None),
        P("ctx", None),
        P("ctx", None),
        P("ctx", None),
        P("ctx", None),
        P("ctx", None),
        P("ctx", None),
        P("ctx", None),
        P("ctx", None),
        P("ctx", None),
        P("ctx", None),
    )
    return jax.shard_map(
        body,
        mesh=mesh,
        in_specs=placed,
        out_specs=(
            P("rep", "ctx", None),
            P("rep", "ctx", None),
            P("ctx", None),
            P("ctx", None),
            P("ctx", None),
            P("ctx", None),
            P("ctx", None),
            P("ctx", None),
            P("ctx", None),
            P("ctx", None),
            P("ctx", None),
            P("ctx", None),
            P("ctx", None),
            P("ctx", None),
            P("ctx", None),
            P("ctx", None),
            P("ctx", None),
            P("ctx", None),
            P("ctx", None),
            P("ctx", None),
            P("ctx", None),
            P("ctx", None),
            P("ctx", None),
            P("ctx", None),
            P("ctx", None),
            P("ctx", None),
        ),
        check_vma=False,
    )
```

time: 3500 us -> 645 us (0.18)
  waiting for transfers between devices: 3030 us -> 0 us
  Pallas kernels: 0 us -> 587 us
  matrix products: 256 us -> 0 us
  local copies, waits for them, and re-layouts: 55 us -> 5.2 us
  blocking collectives: 47.8 us -> 0 us
  other arithmetic: 88.9 us -> 43.9 us
    all_gather x9 -> x0, waiting for transfers between devices: 1450 us -> none  [the longest x1 402 us: body(): lax.all_gather(gate_shard, 'ctx', axis=0, tiled=True)]
    reduce_scatter x8 -> x0, waiting for transfers between devices: 1390 us -> none  [the longest x1 350 us: body(): lax.psum_scatter(product_rows(normed_two, gate_grad_low).astype(jnp.bfloa...]
    pallas_call x0 -> x5, Pallas kernels: none -> 587 us  [the longest x1 167 us: feed_ring(): pl.pallas_call(functools.partial(feed_kernel, n, 256), out_shape=[jax.Sha...]
    dot_general x77 -> x0, matrix products: 256 us -> none  [the longest x7 59.3 us: product_back(): lax.dot_general(left, right, (((1,), (1,)), ((), ())), preferred_element_...]
    psum x1 -> x0, waiting for transfers between devices: 130 us -> none  [body(): lax.psum(query_part.astype(jnp.bfloat16), 'rep').astype(jnp.float32)]
    unnamed x20 -> x0, waiting for transfers between devices: 64.3 us -> none
  transfers between devices with their start and end apart: 19 -> 0, of which waited for: 19 -> 0; matrix products, arithmetic and copies ran while one was open for 6% -> 0% of each run, Pallas kernels for 0% -> 0%
where the time goes in v1:
time: 645 us; the launch traced here: 637 us
  Pallas kernels  587 us (91%)
  other arithmetic  43.9 us (7%)
    pallas_call x1, Pallas kernels, feed_ring(): pl.pallas_call(functools.partial(feed_kernel, n, 256), out_shape=[jax.Sha...  167 us
    pallas_call x1, Pallas kernels, enter(): pl.pallas_call(functools.partial(entry_kernel, n, head_dim), out_shape=[j...  152 us
    pallas_call x1, Pallas kernels, attend(): pl.pallas_call(functools.partial(attend_kernel, n, group, 256), out_shape...  99.5 us
    pallas_call x1, Pallas kernels, attend_back(): pl.pallas_call(functools.partial(attend_back_kernel, n, group, 256), out_...  90.2 us
    pallas_call x1, Pallas kernels, last_sums(): pl.pallas_call(functools.partial(last_kernel, n, widths), out_shape=[jax....  77.5 us
    sub x7, other arithmetic, adamw(): return (weight - rate * (update + decay * weight), first_new, second_new)  36.8 us

profile of v1, /device:TPU:0, one launch (start us, length us, event | category | flops | bytes accessed | tf_op | source)
XLA Modules:
  0.0 637.3 jit_solution(2341978210092795831)
XLA Ops:
  0.7 0.7 convert_bitcast_fusion
  1.4 0.6 pad_convert_fusion.g_ref
  2.0 152.5 %shard_map.467 = (bf16[8,2,128,1536]{3,2,1,0:T(8,128)(2,1)}, f32[5,1024,128]{2,1,0:T(8,128)}, f32[8,8,256]{2,1,0:T(8,128)}, bf16[8,48,1536]{2,1,0:T(8,128)(2,1)}...) custom-call(bf16[256,1536]{1,0:T(8,128)(2,1)} %bitcast.38, ...), custom_call_target="tpu_custom_call" | custom-call | tf_op jit(solution)/shard_map/pallas_call | solution.py:495
  154.4 0.8 slice_bitcast_fusion
  155.3 0.1 reshape.81
  155.4 0.6 slice_bitcast_fusion.3
  156.0 0.1 maximum_bitcast_fusion
  156.1 0.6 select_maximum_fusion.gain_ref
  156.7 99.5 %shard_map.468 = (bf16[5,1024,128]{2,1,0:T(8,128)(2,1)}, f32[3,1024,128]{2,1,0:T(8,128)}, bf16[256,1536]{1,0:T(8,128)(2,1)}, f32[256,1536]{1,0:T(8,128)}, bf16[2...) custom-call(f32[5,1024,128]{2,1,0:T(8,128)} %get-tuple-element.68.lin_ref.lin_src, ...), custom_call_target="tpu_custom_call" | custom-call | flops 6442450944 | bytes 67108864 | tf_op jit(solution)/shard_map/pallas_call | solution.py:772
  256.2 167.0 %shard_map.469 = (bf16[256,768]{1,0:T(8,128)(2,1)}, bf16[8,256,768]{2,1,0:T(8,128)(2,1)}, bf16[256,1536]{1,0:T(8,128)(2,1)}, bf16[8,4,48,2560]{3,2,1,0:T(8,128)(...) custom-call(bf16[256,1536]{1,0:T(8,128)(2,1)} %get-tuple-element.72., ...), custom_call_target="tpu_custom_call" | custom-call | flops 48922361856 | bytes 53084160 | tf_op jit(solution)/shard_map/pallas_call | solution.py:1795
  423.2 90.2 %shard_map.470 = (bf16[8,5,128,128]{3,2,1,0:T(8,128)(2,1)}, bf16[8,2,48,384]{3,2,1,0:T(8,128)(2,1)}, f32[8,128]{1,0:T(8,128)}, bf16[48,6912]{1,0:T(8,128)(2,1)},...) custom-call(bf16[5,1024,128]{2,1,0:T(8,128)(2,1)} %get-tuple-element, ...), custom_call_target="tpu_custom_call" | custom-call | flops 16106127360 | bytes 67108864 | tf_op jit(solution)/shard_map/pallas_call | solution.py:1149
  513.4 1.4 slice.50.f_gain
  514.8 77.5 %shard_map.471 = (f32[256,1536]{1,0:T(8,128)}, f32[32,128]{1,0:T(8,128)}, bf16[256,768]{1,0:T(8,128)(2,1)}, bf16[192,2560]{1,0:T(8,128)(2,1)}, bf16[192,1536]{1,...) custom-call(bf16[256,1536]{1,0:T(8,128)(2,1)} %bitcast.40, ...), custom_call_target="tpu_custom_call" | custom-call | tf_op jit(solution)/shard_map/pallas_call | solution.py:1431
  592.3 0.0 copy-start.19
  592.3 0.0 copy-start.20
  592.3 0.0 copy-start.21
  592.3 0.0 copy-start.5
  592.3 0.0 copy-start.6
  592.4 0.0 copy-start.13
  592.4 0.0 copy-start.14
  592.4 0.0 copy-start.15
  592.4 0.0 copy-start.16
  592.4 2.2 add_convert_fusion
  594.7 2.9 add.116
  597.6 0.1 fusion.31
  597.7 0.0 copy-done.19
  597.7 0.0 copy-done.20
  597.7 0.0 copy-done.21
  597.7 0.7 multiply_subtract_fusion.7
  598.4 0.0 copy-done.6
  598.5 0.0 copy-start.1
  598.5 0.0 copy-start.9
  598.5 0.0 copy-start.10
  598.5 0.0 slice-start.6
  598.5 1.8 multiply_subtract_fusion.5
  600.3 0.0 slice-start
  600.4 0.0 slice-start.7
  600.4 2.4 multiply_subtract_fusion.4
  602.8 0.0 slice-start.1
  602.8 0.0 slice-start.2
  602.8 2.4 multiply_subtract_fusion.3
  605.3 1.4 slice-done
  606.7 0.2 slice-done.7
  606.9 0.4 slice-done.1
  607.3 9.3 %multiply_subtract_fusion.2 = (f32[192,6912]{1,0:T(8,128)}, f32[192,6912]{1,0:T(8,128)}, f32[192,6912]{1,0:T(8,128)}) fusion(f32[192,6912]{1,0:T(8,128)S(1)} %bitcast.31, bf16[192,6912]{1,0:T(8,128)(2,1)} %get-tuple-element.106, f32[192,6912]{1,0:T(8,128)S(1)} %bitcast.37, f32[192,6912]{1,0:T(8,128)} %param.50), kind=kLoop, calls=%fused_computation.14 | loop fusion | flops 21233664 | bytes 34504704 | tf_op jit(solution)/shard_map/sub | solution.py:103
  616.6 0.0 slice-start.5
  616.7 10.4 %multiply_subtract_fusion.1 = (f32[192,6912]{1,0:T(8,128)}, f32[192,6912]{1,0:T(8,128)}, f32[192,6912]{1,0:T(8,128)}) fusion(f32[192,6912]{1,0:T(8,128)S(1)} %bitcast.33, bf16[192,6912]{1,0:T(8,128)(2,1)} %get-tuple-element.107, f32[192,6912]{1,0:T(8,128)} %param.43, f32[192,6912]{1,0:T(8,128)} %param.51), kind=kLoop, calls=%fused_computation.13 | loop fusion | flops 21233664 | bytes 34504704 | tf_op jit(solution)/shard_map/sub | solution.py:103
  627.1 9.7 %multiply_subtract_fusion = (f32[864,1536]{1,0:T(8,128)}, f32[864,1536]{1,0:T(8,128)}, f32[864,1536]{1,0:T(8,128)}) fusion(f32[864,1536]{1,0:T(8,128)S(1)} %bitcast.35, bf16[864,1536]{1,0:T(8,128)(2,1)S(1)} %copy-done.2, f32[864,1536]{1,0:T(8,128)} %param.44, f32[864,1536]{1,0:T(8,128)} %param.52), kind=kLoop, calls=%fused_computation.12 | loop fusion | flops 21233664 | bytes 34504704 | tf_op jit(solution)/shard_map/sub | solution.py:103
  (46 shorter events, 0.1 us)
Async XLA Ops:
  514.8 77.6 %copy-start.3 = (f32[256,1536]{1,0:T(8,128)S(1)}, f32[256,1536]{1,0:T(8,128)}, u32[]{:S(2)}) copy-start(f32[256,1536]{1,0:T(8,128)} %get-tuple-element.71.r_ref) | copy-start | bytes 4718596
  514.8 77.6 %copy-start.17 = (bf16[256,768]{1,0:T(8,128)(2,1)S(1)}, bf16[256,768]{1,0:T(8,128)(2,1)}, u32[]{:S(2)}) copy-start(bf16[256,768]{1,0:T(8,128)(2,1)} %get-tuple-element.78) | copy-start | bytes 1179652
  514.8 79.8 %copy-start.4 = (f32[256,1536]{1,0:T(8,128)S(1)}, f32[256,1536]{1,0:T(8,128)}, u32[]{:S(2)}) copy-start(f32[256,1536]{1,0:T(8,128)} %get-tuple-element.102) | copy-start | bytes 4718596
  592.3 5.3 copy-start.18
  592.3 5.4 copy-start.19
  592.3 5.4 copy-start.20
  592.3 5.4 copy-start.21
  592.3 6.1 copy-start.5
  592.3 6.1 copy-start.6
  592.4 6.0 copy-start.11
  592.4 6.0 copy-start.13
  592.4 6.0 copy-start.14
  592.4 6.0 copy-start.15
  592.4 6.0 copy-start.16
  594.6 5.7 copy-start
  594.6 5.7 copy-start.7
  594.6 5.7 copy-start.8
  598.5 4.4 copy-start.1
  598.5 4.3 copy-start.9
  598.5 4.3 copy-start.10
  598.5 4.3 copy-start.12
  598.5 6.8 %slice-start.6 = ((s8[5308416]{0:T(1024)(128)(4,1)}), s8[4194304]{0:T(1024)(128)(4,1)S(1)}, s32[]{:S(2)}) async-start(s8[5308416]{0:T(1024)(128)(4,1)} %bitcast.36), calls=%async_computation.6 | async-start | bytes 8388608
  600.3 6.3 slice-start
  600.4 6.6 %slice-start.7 = ((s8[5308416]{0:T(1024)(128)(4,1)}), s8[1114112]{0:T(1024)(128)(4,1)S(1)}, s32[]{:S(2)}) async-start(s8[5308416]{0:T(1024)(128)(4,1)} %bitcast.36), calls=%async_computation.7 | async-start | bytes 2228224
  602.8 4.5 slice-start.1
  602.8 13.8 %slice-start.2 = ((s8[5308416]{0:T(1024)(128)(4,1)}), s8[4194304]{0:T(1024)(128)(4,1)S(1)}, s32[]{:S(2)}) async-start(s8[5308416]{0:T(1024)(128)(4,1)} %bitcast.32), calls=%async_computation.2 | async-start | bytes 8388608
  607.3 9.4 %slice-start.3 = ((s8[5308416]{0:T(1024)(128)(4,1)}), s8[1114112]{0:T(1024)(128)(4,1)S(1)}, s32[]{:S(2)}) async-start(s8[5308416]{0:T(1024)(128)(4,1)} %bitcast.32), calls=%async_computation.3 | async-start | bytes 2228224
  607.3 19.8 %slice-start.4 = ((s8[5308416]{0:T(1024)(128)(4,1)}), s8[4194304]{0:T(1024)(128)(4,1)S(1)}, s32[]{:S(2)}) async-start(s8[5308416]{0:T(1024)(128)(4,1)} %bitcast.34), calls=%async_computation.4 | async-start | bytes 8388608
  616.6 10.4 %slice-start.5 = ((s8[5308416]{0:T(1024)(128)(4,1)}), s8[1114112]{0:T(1024)(128)(4,1)S(1)}, s32[]{:S(2)}) async-start(s8[5308416]{0:T(1024)(128)(4,1)} %bitcast.34), calls=%async_computation.5 | async-start | bytes 2228224
  616.7 10.4 %copy-start.2 = (bf16[864,1536]{1,0:T(8,128)(2,1)S(1)}, bf16[864,1536]{1,0:T(8,128)(2,1)}, u32[]{:S(2)}) copy-start(bf16[864,1536]{1,0:T(8,128)(2,1)} %get-tuple-element.108) | copy-start | bytes 7962628

commit v2 on v1

--- a/solution.py
+++ b/solution.py
@@ -319,8 +319,8 @@
         block = target.at[(owner_of(step, up),) + where]
         remote(block, block, x_send.at[at, step], x_recv.at[at, step], right).wait_recv()
 
-    def pass_first(step):
-        for at in range(len(pieces)):
+    def pass_first(which, step):
+        for at in which:
             arrived(at, step)
             hop_copy(at, step).start()
 
@@ -379,6 +379,7 @@
     own[5].start()
     for hop in range(1, n):
         swap_copy(2, hop).start()
+    pass_first(tokens, 0)
     for copy in loads[:3]:
         copy.wait()
     for source, at, wide in ((wq, 0, wq.shape[1] // n), (wk, 1, head_dim), (wv, 2, head_dim)):
@@ -400,7 +401,6 @@
     own[4].start()
     for at in weights:
         hop_copy(at, -1).start()
-    pass_first(0)
     loads[6].wait()
 
     @pl.loop(0, wd.shape[0] // 16)
@@ -410,6 +410,8 @@
 
     wd_give = pltpu.make_async_copy(wd_low, wd_out, own_sem.at[6])
     wd_give.start()
+    pass_first(weights, 0)
+    pass_first(tokens, 1)
     for hop in range(1, n):
         swap_copy(0, hop).wait_recv()
         swap_copy(1, hop).wait_recv()
@@ -442,7 +444,10 @@
 
     @pl.loop(0, n - 1)
     def _(step):
-        pass_on(tokens, step + 1)
+        @pl.when(step > 0)
+        def _():
+            pass_on(tokens, step + 1)
+
         multiply(step, 0)
         pass_on(weights, step + 1)
 
@@ -678,6 +683,8 @@
             if head == group:
                 low_out[group + 1, here] = lin_ref[group + 1, here].astype(low)
 
+    served = list(range(1, group * (length // block), 2))[: n - 1]
+
     @pl.loop(0, group)
     def _(head):
         for at in range(length // block):
@@ -694,12 +701,18 @@
                 sums.append(jnp.broadcast_to(top + jnp.log(total), (block, low_out.shape[2])))
             o_own[head, here] = pack(*outs).astype(low)
             lse_out[head, here] = pack(*sums)
-            for unit in range(2, group * (length // block), 3):
+            for hop, unit in enumerate(served):
                 if unit % (length // block) == at:
 
                     @pl.when(head == unit // (length // block))
-                    def _(unit=unit):
-                        hop_on(unit // 3)
+                    def _(hop=hop):
+                        hop_on(hop)
+
+            if at == 0:
+
+                @pl.when(head == group - 1)
+                def _():
+                    share.middle()
 
         for hop in range(1, n):
             give(head, hop).start()
@@ -712,16 +725,7 @@
     ]
     gives[0].start()
     gives[1].start()
-    served = group * (length // block) // 3
-    middle = served + 1
-
-    @pl.loop(served, middle)
-    def _(step):
-        hop_on(step)
-
-    share.middle()
-
-    @pl.loop(middle, n - 1)
+    @pl.loop(len(served), n - 1)
     def _(step):
         hop_on(step)
 

time: 645 us -> 646 us (level)
    pallas_call x1, Pallas kernels: 152 us -> 160 us  [enter(): pl.pallas_call(functools.partial(entry_kernel, n, head_dim), out_shape=[j...]
    pallas_call x1, Pallas kernels: 99.5 us -> 92.4 us  [attend(): pl.pallas_call(functools.partial(attend_kernel, n, group, 256), out_shape...]
where the time goes in v2:
time: 646 us; the launch traced here: 639 us
  Pallas kernels  588 us (91%)
  other arithmetic  43.9 us (7%)
    pallas_call x1, Pallas kernels, feed_ring(): pl.pallas_call(functools.partial(feed_kernel, n, 256), out_shape=[jax.Sha...  168 us
    pallas_call x1, Pallas kernels, enter(): pl.pallas_call(functools.partial(entry_kernel, n, head_dim), out_shape=[j...  160 us
    pallas_call x1, Pallas kernels, attend(): pl.pallas_call(functools.partial(attend_kernel, n, group, 256), out_shape...  92.4 us
    pallas_call x1, Pallas kernels, attend_back(): pl.pallas_call(functools.partial(attend_back_kernel, n, group, 256), out_...  89.2 us
    pallas_call x1, Pallas kernels, last_sums(): pl.pallas_call(functools.partial(last_kernel, n, widths), out_shape=[jax....  78.7 us
    sub x7, other arithmetic, adamw(): return (weight - rate * (update + decay * weight), first_new, second_new)  36.8 us

profile of v2, /device:TPU:0, one launch (start us, length us, event | category | flops | bytes accessed | tf_op | source)
XLA Modules:
  0.0 638.9 jit_solution(7543614689768482152)
XLA Ops:
  0.7 0.7 convert_bitcast_fusion
  1.4 0.6 pad_convert_fusion.g_ref
  2.0 159.6 %shard_map.467 = (bf16[8,2,128,1536]{3,2,1,0:T(8,128)(2,1)}, f32[5,1024,128]{2,1,0:T(8,128)}, f32[8,8,256]{2,1,0:T(8,128)}, bf16[8,48,1536]{2,1,0:T(8,128)(2,1)}...) custom-call(bf16[256,1536]{1,0:T(8,128)(2,1)} %bitcast.38, ...), custom_call_target="tpu_custom_call" | custom-call | tf_op jit(solution)/shard_map/pallas_call | solution.py:500
  161.6 0.8 slice_bitcast_fusion
  162.4 0.1 reshape.81
  162.5 0.6 slice_bitcast_fusion.3
  163.1 0.1 maximum_bitcast_fusion
  163.2 0.6 select_maximum_fusion.gain_ref
  163.8 92.4 %shard_map.468 = (bf16[5,1024,128]{2,1,0:T(8,128)(2,1)}, f32[3,1024,128]{2,1,0:T(8,128)}, bf16[256,1536]{1,0:T(8,128)(2,1)}, f32[256,1536]{1,0:T(8,128)}, bf16[2...) custom-call(f32[5,1024,128]{2,1,0:T(8,128)} %get-tuple-element.68.lin_ref.lin_src, ...), custom_call_target="tpu_custom_call" | custom-call | flops 6442450944 | bytes 67108864 | tf_op jit(solution)/shard_map/pallas_call | solution.py:776
  256.3 168.4 %shard_map.469 = (bf16[256,768]{1,0:T(8,128)(2,1)}, bf16[8,256,768]{2,1,0:T(8,128)(2,1)}, bf16[256,1536]{1,0:T(8,128)(2,1)}, bf16[8,4,48,2560]{3,2,1,0:T(8,128)(...) custom-call(bf16[256,1536]{1,0:T(8,128)(2,1)} %get-tuple-element.72., ...), custom_call_target="tpu_custom_call" | custom-call | flops 48922361856 | bytes 53084160 | tf_op jit(solution)/shard_map/pallas_call | solution.py:1799
  424.7 89.2 %shard_map.470 = (bf16[8,5,128,128]{3,2,1,0:T(8,128)(2,1)}, bf16[8,2,48,384]{3,2,1,0:T(8,128)(2,1)}, f32[8,128]{1,0:T(8,128)}, bf16[48,6912]{1,0:T(8,128)(2,1)},...) custom-call(bf16[5,1024,128]{2,1,0:T(8,128)(2,1)} %get-tuple-element, ...), custom_call_target="tpu_custom_call" | custom-call | flops 16106127360 | bytes 67108864 | tf_op jit(solution)/shard_map/pallas_call | solution.py:1153
  513.8 1.4 slice.50.f_gain
  515.2 78.7 %shard_map.471 = (f32[256,1536]{1,0:T(8,128)}, f32[32,128]{1,0:T(8,128)}, bf16[256,768]{1,0:T(8,128)(2,1)}, bf16[192,2560]{1,0:T(8,128)(2,1)}, bf16[192,1536]{1,...) custom-call(bf16[256,1536]{1,0:T(8,128)(2,1)} %bitcast.40, ...), custom_call_target="tpu_custom_call" | custom-call | tf_op jit(solution)/shard_map/pallas_call | solution.py:1435
  594.0 0.0 copy-start.19
  594.0 0.0 copy-start.20
  594.0 0.0 copy-start.21
  594.0 0.0 copy-start.5
  594.0 0.0 copy-start.6
  594.0 0.0 copy-start.13
  594.0 0.0 copy-start.14
  594.1 0.0 copy-start.15
  594.1 0.0 copy-start.16
  594.1 2.2 add_convert_fusion
  596.3 2.9 add.116
  599.2 0.1 fusion.31
  599.3 0.0 copy-done.19
  599.4 0.0 copy-done.20
  599.4 0.0 copy-done.21
  599.4 0.7 multiply_subtract_fusion.7
  600.1 0.0 copy-done.6
  600.1 0.0 copy-start.1
  600.1 0.0 copy-start.9
  600.1 0.0 copy-start.10
  600.2 0.0 slice-start.6
  600.2 1.8 multiply_subtract_fusion.5
  602.0 0.0 slice-start
  602.0 0.0 slice-start.7
  602.0 2.4 multiply_subtract_fusion.4
  604.5 0.0 slice-start.1
  604.5 0.0 slice-start.2
  604.5 2.4 multiply_subtract_fusion.3
  606.9 1.4 slice-done
  608.3 0.2 slice-done.7
  608.6 0.4 slice-done.1
  608.9 9.3 %multiply_subtract_fusion.2 = (f32[192,6912]{1,0:T(8,128)}, f32[192,6912]{1,0:T(8,128)}, f32[192,6912]{1,0:T(8,128)}) fusion(f32[192,6912]{1,0:T(8,128)S(1)} %bitcast.31, bf16[192,6912]{1,0:T(8,128)(2,1)} %get-tuple-element.106, f32[192,6912]{1,0:T(8,128)S(1)} %bitcast.37, f32[192,6912]{1,0:T(8,128)} %param.50), kind=kLoop, calls=%fused_computation.14 | loop fusion | flops 21233664 | bytes 34504704 | tf_op jit(solution)/shard_map/sub | solution.py:103
  618.3 0.0 slice-start.5
  618.3 10.4 %multiply_subtract_fusion.1 = (f32[192,6912]{1,0:T(8,128)}, f32[192,6912]{1,0:T(8,128)}, f32[192,6912]{1,0:T(8,128)}) fusion(f32[192,6912]{1,0:T(8,128)S(1)} %bitcast.33, bf16[192,6912]{1,0:T(8,128)(2,1)} %get-tuple-element.107, f32[192,6912]{1,0:T(8,128)} %param.43, f32[192,6912]{1,0:T(8,128)} %param.51), kind=kLoop, calls=%fused_computation.13 | loop fusion | flops 21233664 | bytes 34504704 | tf_op jit(solution)/shard_map/sub | solution.py:103
  628.7 9.7 %multiply_subtract_fusion = (f32[864,1536]{1,0:T(8,128)}, f32[864,1536]{1,0:T(8,128)}, f32[864,1536]{1,0:T(8,128)}) fusion(f32[864,1536]{1,0:T(8,128)S(1)} %bitcast.35, bf16[864,1536]{1,0:T(8,128)(2,1)S(1)} %copy-done.2, f32[864,1536]{1,0:T(8,128)} %param.44, f32[864,1536]{1,0:T(8,128)} %param.52), kind=kLoop, calls=%fused_computation.12 | loop fusion | flops 21233664 | bytes 34504704 | tf_op jit(solution)/shard_map/sub | solution.py:103
  (46 shorter events, 0.1 us)
Async XLA Ops:
  515.2 78.8 %copy-start.3 = (f32[256,1536]{1,0:T(8,128)S(1)}, f32[256,1536]{1,0:T(8,128)}, u32[]{:S(2)}) copy-start(f32[256,1536]{1,0:T(8,128)} %get-tuple-element.71.r_ref) | copy-start | bytes 4718596
  515.2 78.9 %copy-start.17 = (bf16[256,768]{1,0:T(8,128)(2,1)S(1)}, bf16[256,768]{1,0:T(8,128)(2,1)}, u32[]{:S(2)}) copy-start(bf16[256,768]{1,0:T(8,128)(2,1)} %get-tuple-element.78) | copy-start | bytes 1179652
  515.2 81.1 %copy-start.4 = (f32[256,1536]{1,0:T(8,128)S(1)}, f32[256,1536]{1,0:T(8,128)}, u32[]{:S(2)}) copy-start(f32[256,1536]{1,0:T(8,128)} %get-tuple-element.102) | copy-start | bytes 4718596
  594.0 5.3 copy-start.18
  594.0 5.4 copy-start.19
  594.0 5.4 copy-start.20
  594.0 5.4 copy-start.21
  594.0 6.1 copy-start.5
  594.0 6.1 copy-start.6
  594.0 6.0 copy-start.11
  594.0 6.0 copy-start.13
  594.0 6.0 copy-start.14
  594.1 6.0 copy-start.15
  594.1 6.0 copy-start.16
  596.3 5.7 copy-start
  596.3 5.7 copy-start.7
  596.3 5.7 copy-start.8
  600.1 4.4 copy-start.1
  600.1 4.3 copy-start.9
  600.1 4.3 copy-start.10
  600.1 4.3 copy-start.12
  600.2 6.8 %slice-start.6 = ((s8[5308416]{0:T(1024)(128)(4,1)}), s8[4194304]{0:T(1024)(128)(4,1)S(1)}, s32[]{:S(2)}) async-start(s8[5308416]{0:T(1024)(128)(4,1)} %bitcast.36), calls=%async_computation.6 | async-start | bytes 8388608
  602.0 6.3 slice-start
  602.0 6.6 %slice-start.7 = ((s8[5308416]{0:T(1024)(128)(4,1)}), s8[1114112]{0:T(1024)(128)(4,1)S(1)}, s32[]{:S(2)}) async-start(s8[5308416]{0:T(1024)(128)(4,1)} %bitcast.36), calls=%async_computation.7 | async-start | bytes 2228224
  604.5 4.5 slice-start.1
  604.5 13.8 %slice-start.2 = ((s8[5308416]{0:T(1024)(128)(4,1)}), s8[4194304]{0:T(1024)(128)(4,1)S(1)}, s32[]{:S(2)}) async-start(s8[5308416]{0:T(1024)(128)(4,1)} %bitcast.32), calls=%async_computation.2 | async-start | bytes 8388608
  608.9 9.4 %slice-start.3 = ((s8[5308416]{0:T(1024)(128)(4,1)}), s8[1114112]{0:T(1024)(128)(4,1)S(1)}, s32[]{:S(2)}) async-start(s8[5308416]{0:T(1024)(128)(4,1)} %bitcast.32), calls=%async_computation.3 | async-start | bytes 2228224
  608.9 19.8 %slice-start.4 = ((s8[5308416]{0:T(1024)(128)(4,1)}), s8[4194304]{0:T(1024)(128)(4,1)S(1)}, s32[]{:S(2)}) async-start(s8[5308416]{0:T(1024)(128)(4,1)} %bitcast.34), calls=%async_computation.4 | async-start | bytes 8388608
  618.3 10.4 %slice-start.5 = ((s8[5308416]{0:T(1024)(128)(4,1)}), s8[1114112]{0:T(1024)(128)(4,1)S(1)}, s32[]{:S(2)}) async-start(s8[5308416]{0:T(1024)(128)(4,1)} %bitcast.34), calls=%async_computation.5 | async-start | bytes 2228224
  618.3 10.4 %copy-start.2 = (bf16[864,1536]{1,0:T(8,128)(2,1)S(1)}, bf16[864,1536]{1,0:T(8,128)(2,1)}, u32[]{:S(2)}) copy-start(bf16[864,1536]{1,0:T(8,128)(2,1)} %get-tuple-element.108) | copy-start | bytes 7962628
